TPU v7x, 256 devices: a whole 4x4x8 slice. The times are simulated.
256 devices in a mesh: lat: 16 (over y, x_hi, core), lon: 16 (over x_lo, z).
Axes of the slice: x: 4 (x_hi: 2, x_lo: 2; x = x_hi * 2 + x_lo), y: 4, z: 8, core: 2. Of those that a mesh axis runs over, the one named last changes fastest.
Arguments:
- inputs: bfloat16 [2, 96, 192, 384], P(None, 'lat', 'lon'), may hold values from -6 to 6
- cotangent: bfloat16 [2, 96, 192, 384], P(None, 'lat', 'lon'), may hold values from -6 to 6
- norm_gain: float32 [384], replicated, may hold values from 0.1 to 1.9
- qkv_weight: bfloat16 [384, 1152], replicated, may hold values from -8 to 8
- proj_weight: bfloat16 [384, 384], replicated, may hold values from -0.3125 to 0.3125
- bias_table: bfloat16 [32, 12, 3312], replicated, may hold values from -4 to 320
- window_type: int32 [16, 1], P('lat'), may hold values from 0 to 31
- region: int32 [2, 96, 192], P(None, 'lat', 'lon'), may hold values from 0 to 2
Outputs:
- block_out: bfloat16 [2, 96, 192, 384], P(None, 'lat', 'lon')
- grad_inputs: bfloat16 [2, 96, 192, 384], P(None, 'lat', 'lon')
- grad_gain: float32 [384], replicated
- grad_qkv: float32 [384, 1152], P('lat', 'lon')
- grad_proj: float32 [384, 384], P('lat', 'lon')
- grad_bias: float32 [32, 12, 3312], P('lat', None, 'lon')
All inputs are finite; a program needn't handle non-finite values.
Results may differ from a plain program's by a relative error of at most 0.0088.
Values may be sent and summed in bfloat16 or wider, within the bound.
A program may use at most 128 MiB of HBM per device.

v0:
```python
import jax
import jax.numpy as jnp
import numpy as np
from jax import lax
from jax.sharding import PartitionSpec as P


def from_behind(value, axis, by):
    devices = lax.axis_size(axis)
    return lax.ppermute(value, axis, [(i, (i + by) % devices) for i in range(devices)])


def offset_table():
    col_pos = np.arange(12)
    offset = col_pos[:, None] - col_pos[None, :] + 11
    table = (np.arange(23)[:, None, None] == offset[None, :, :]).astype(np.float32)
    return jnp.asarray(table)


def to_windows(block_in):
    levels, row_count, col_count, feature_count = block_in.shape
    tiled_grid = block_in.reshape(
        levels // 2, 2, row_count // 6, 6, col_count // 12, 12, feature_count
    )
    tiled_grid = tiled_grid.transpose(0, 2, 4, 1, 3, 5, 6)
    return tiled_grid.reshape(-1, 144, feature_count)


def from_windows(windows, levels, row_count, col_count):
    feature_count = windows.shape[-1]
    tiled_grid = windows.reshape(
        levels // 2, row_count // 6, col_count // 12, 2, 6, 12, feature_count
    )
    return tiled_grid.transpose(0, 3, 1, 4, 2, 5, 6).reshape(
        levels, row_count, col_count, feature_count
    )


def product(pattern, left_op, right_op):
    return jnp.einsum(pattern, left_op, right_op, preferred_element_type=jnp.float32)


def window_pass(inputs, cotangent, cell_key, norm_gain, qkv_weight, proj_weight, bias_rows):
    win_count, tokens_win, model_width = inputs.shape
    head_count = bias_rows.shape[1]
    head_dim = model_width // head_count
    score_scale = head_dim ** (-0.5)
    wide_in = inputs.reshape(-1, model_width).astype(jnp.float32)
    center = jnp.mean(wide_in, -1, keepdims=True)
    spread = jnp.mean(jnp.square(wide_in - center), -1, keepdims=True)
    inv_std = lax.rsqrt(spread + 1e-05)
    normed = (wide_in - center) * inv_std
    hidden = (normed * norm_gain).astype(jnp.bfloat16)
    joined_qkv = jnp.dot(hidden, qkv_weight, preferred_element_type=jnp.float32).astype(
        jnp.bfloat16
    )
    joined_qkv = joined_qkv.reshape(win_count, tokens_win, 3, head_count, head_dim)
    queries = joined_qkv[:, :, 0]
    key_rows = joined_qkv[:, :, 1]
    value_rows = joined_qkv[:, :, 2]
    spread_table = offset_table()
    bias_parts = bias_rows.reshape(win_count, head_count, 2, 2, 6, 6, 23)
    bias_full = jnp.einsum(
        "whabcdo,oef->whacebdf", bias_parts, spread_table, precision=lax.Precision.HIGHEST
    )
    bias_full = bias_full.reshape(win_count, head_count, tokens_win, tokens_win)
    scores = product("wqhd,wkhd->whqk", queries, key_rows) * score_scale + bias_full
    allowed = (cell_key[:, :, None] == cell_key[:, None, :])[:, None]
    scores = jnp.where(allowed, scores, -1e30)
    row_top = jnp.max(scores, -1, keepdims=True)
    exp_scores = jnp.exp(scores - row_top)
    probs_full = exp_scores / jnp.sum(exp_scores, -1, keepdims=True)
    probs_low = probs_full.astype(jnp.bfloat16)
    attended = (
        product("whqk,wkhd->wqhd", probs_low, value_rows)
        .astype(jnp.bfloat16)
        .reshape(-1, model_width)
    )
    branch = jnp.dot(attended, proj_weight, preferred_element_type=jnp.float32)
    result = (wide_in + branch).astype(jnp.bfloat16)
    grad_flat = cotangent.reshape(-1, model_width)
    grad_proj = jnp.dot(attended.T, grad_flat, preferred_element_type=jnp.float32)
    grad_att = jnp.dot(grad_flat, proj_weight.T, preferred_element_type=jnp.float32).astype(
        jnp.bfloat16
    )
    grad_att = grad_att.reshape(win_count, tokens_win, head_count, head_dim)
    grad_probs = product("wqhd,wkhd->whqk", grad_att, value_rows)
    grad_values = product("whqk,wqhd->wkhd", probs_low, grad_att)
    grad_scores = probs_full * (grad_probs - jnp.sum(probs_full * grad_probs, -1, keepdims=True))
    score_parts = grad_scores.reshape(win_count, head_count, 2, 6, 12, 2, 6, 12)
    grad_bias = jnp.einsum(
        "whacebdf,oef->whabcdo", score_parts, spread_table, precision=lax.Precision.HIGHEST
    )
    grad_bias = grad_bias.reshape(win_count, head_count, bias_rows.shape[2])
    grad_scaled = (grad_scores * score_scale).astype(jnp.bfloat16)
    grad_query = product("whqk,wkhd->wqhd", grad_scaled, key_rows)
    grad_keys = product("whqk,wqhd->wkhd", grad_scaled, queries)
    grad_joined = (
        jnp.stack([grad_query, grad_keys, grad_values], 2)
        .astype(jnp.bfloat16)
        .reshape(-1, 3 * model_width)
    )
    grad_qkv = jnp.dot(hidden.T, grad_joined, preferred_element_type=jnp.float32)
    grad_hidden = jnp.dot(grad_joined, qkv_weight.T, preferred_element_type=jnp.float32)
    grad_gain = jnp.sum(grad_hidden * normed, 0)
    grad_normed = grad_hidden * norm_gain
    grad_wide = inv_std * (
        grad_normed
        - jnp.mean(grad_normed, -1, keepdims=True)
        - normed * jnp.mean(grad_normed * normed, -1, keepdims=True)
    )
    grad_in = (grad_flat.astype(jnp.float32) + grad_wide).astype(jnp.bfloat16)
    return (
        result.reshape(inputs.shape),
        grad_in.reshape(inputs.shape),
        grad_qkv,
        grad_proj,
        grad_gain,
        grad_bias,
    )


def into_frame(block_in):
    block_in = jnp.roll(block_in, -1, axis=0)
    upper_rim = from_behind(block_in[:, :3], "lat", -1)
    block_in = jnp.concatenate([block_in[:, 3:], upper_rim], 1)
    side_rim = from_behind(block_in[:, :, :6], "lon", -1)
    return jnp.concatenate([block_in[:, :, 6:], side_rim], 2)


def out_of_frame(block_in):
    side_rim = from_behind(block_in[:, :, -6:], "lon", 1)
    block_in = jnp.concatenate([side_rim, block_in[:, :, :-6]], 2)
    lower_rim = from_behind(block_in[:, -3:], "lat", 1)
    block_in = jnp.concatenate([lower_rim, block_in[:, :-3]], 1)
    return jnp.roll(block_in, 1, axis=0)


def local(inputs, cotangent, norm_gain, qkv_weight, proj_weight, bias_table, window_type, region):
    levels, lat_dev, lon_dev, model_width = inputs.shape
    lat_index = lax.axis_index("lat")
    lon_index = lax.axis_index("lon")
    lat_count = lax.axis_size("lat")
    lon_count = lax.axis_size("lon")
    framed_in = into_frame(inputs)
    framed_cot = into_frame(cotangent)
    row_ids = lat_dev * lat_index + jnp.arange(lat_dev, dtype=jnp.int32)
    lat_side = (row_ids + 3 >= lat_dev * lat_count).astype(jnp.int32)
    lev_side = (jnp.arange(levels, dtype=jnp.int32) + 1 >= levels).astype(jnp.int32)
    key_grid = region * 4 + lat_side[None, :, None] * 2 + lev_side[:, None, None]
    type_count, head_count, rel_count = bias_table.shape
    per_window = window_type.T[:, :, None].reshape(-1)
    onehot = (per_window[:, None] == jnp.arange(type_count, dtype=jnp.int32)[None, :]).astype(
        jnp.bfloat16
    )
    bias_rows = jnp.dot(
        onehot, bias_table.reshape(type_count, -1), preferred_element_type=jnp.float32
    )
    bias_rows = bias_rows.reshape(per_window.shape[0], head_count, rel_count)
    pieces = window_pass(
        to_windows(framed_in),
        to_windows(framed_cot),
        to_windows(key_grid[..., None])[..., 0],
        norm_gain,
        qkv_weight,
        proj_weight,
        bias_rows,
    )
    result_win, grad_win, grad_qkv, grad_proj, grad_gain, grad_bias_win = pieces
    result_block = from_windows(result_win, levels, lat_dev, lon_dev)
    grad_block = from_windows(grad_win, levels, lat_dev, lon_dev)
    block_out = out_of_frame(result_block)
    grad_inputs = out_of_frame(grad_block)
    grad_bias = jnp.einsum(
        "wt,whr->thr", onehot.astype(jnp.float32), grad_bias_win, precision=lax.Precision.HIGHEST
    )
    grad_bias, grad_qkv, grad_proj, grad_gain = lax.psum(
        (grad_bias, grad_qkv, grad_proj, grad_gain), ("lat", "lon")
    )
    type_share = type_count // lat_count
    rel_share = rel_count // lon_count
    width_lat = model_width // lat_count
    qkv_share = 3 * model_width // lon_count
    proj_share = model_width // lon_count
    grad_bias = lax.dynamic_slice_in_dim(grad_bias, lat_index * type_share, type_share, 0)
    grad_bias = lax.dynamic_slice_in_dim(grad_bias, lon_index * rel_share, rel_share, 2)
    grad_qkv = lax.dynamic_slice_in_dim(grad_qkv, lat_index * width_lat, width_lat, 0)
    grad_qkv = lax.dynamic_slice_in_dim(grad_qkv, lon_index * qkv_share, qkv_share, 1)
    grad_proj = lax.dynamic_slice_in_dim(grad_proj, lat_index * width_lat, width_lat, 0)
    grad_proj = lax.dynamic_slice_in_dim(grad_proj, lon_index * proj_share, proj_share, 1)
    return (block_out, grad_inputs, grad_gain, grad_qkv, grad_proj, grad_bias)


def solution(mesh):
    return jax.shard_map(
        local,
        mesh=mesh,
        in_specs=(
            P(None, "lat", "lon", None),
            P(None, "lat", "lon", None),
            P(),
            P(),
            P(),
            P(),
            P("lat", None),
            P(None, "lat", "lon"),
        ),
        out_specs=(
            P(None, "lat", "lon", None),
            P(None, "lat", "lon", None),
            P(),
            P("lat", "lon"),
            P("lat", "lon"),
            P("lat", None, "lon"),
        ),
        check_vma=False,
    )
```

profile of v0, /device:TPU:1, one launch (start us, length us, event | category | flops | bytes accessed | tf_op | source)
XLA Modules:
  0.0 504.1 jit_solution(8356594696503716648)
XLA Ops:
  9.3 3.2 collective-permute-start
  14.6 3.7 collective-permute-start.4
  18.3 4.9 copy.58
  23.2 5.6 %reshape.379 = bf16[32,39744]{1,0:T(8,128)(2,1)S(1)} reshape(bf16[32,12,3312]{2,1,0:T(8,128)(2,1)} %copy.58) | data formatting | bytes 5087232 | tf_op jit(solution)/shard_map/reshape | solution.py:157
  28.8 7.2 %copy.59 = bf16[39744,32]{1,0:T(8,128)(2,1)} copy(bf16[39744,32]{0,1:T(8,128)(2,1)S(1)} %bitcast.93) | data formatting | bytes 5087232 | tf_op jit(solution)/shard_map/dot_general | solution.py:156
  36.0 16.3 %reshape.380 = bf16[12,2,2,6,6,23,32]{6,5,4,3,2,1,0:T(8,128)(2,1)} reshape(bf16[39744,32]{1,0:T(8,128)(2,1)} %copy.59) | data formatting | bytes 5087232 | tf_op jit(solution)/shard_map/reshape.143
  53.8 21.4 %fusion.30 = f32[1,12,2,2,6,6,23]{6,0,5,4,3,2,1:T(1,128)S(1)} fusion(bf16[12,2,2,6,6,23,32]{6,5,4,3,2,1,0:T(8,128)(2,1)} %reshape.380, s32[]{:T(128)} %bitcast.92), kind=kOutput, calls=%fused_computation.75 | convolution fusion | flops 2543648 | bytes 2702596 | tf_op jit(solution)/shard_map/dot_general | solution.py:156
  75.2 13.9 %convolution_bitcast_fusion = f32[1,12,2,6,12,2,6,12]{1,7,6,3,5,2,4,0:T(8,128)} fusion(f32[23,12,12,1,1,1,1]{0,2,6,5,4,3,1:T(8,128)S(1)} %copy-done.15, f32[1,12,2,2,6,6,23]{6,0,5,4,3,2,1:T(1,128)S(1)} %fusion.30), kind=kOutput, calls=%fused_computation.2 | convolution fusion | flops 68677632 | bytes 1167552 | tf_op jit(solution)/shard_map/whabcdo,oef->whacebdf/dot_general | solution.py:63
  89.1 21.6 %copy.83 = f32[1,12,2,6,12,2,6,12]{4,3,2,7,6,5,1,0:T(8,128)} copy(f32[1,12,2,6,12,2,6,12]{1,7,6,3,5,2,4,0:T(8,128)} %convolution_bitcast_fusion) | data formatting | bytes 1990656 | tf_op jit(solution)/shard_map/reshape | solution.py:66
  110.7 10.2 %reshape.392 = f32[12,144,144]{1,2,0:T(8,128)} reshape(f32[1,12,2,6,12,2,6,12]{4,3,2,7,6,5,1,0:T(8,128)} %copy.83) | data formatting | bytes 1990656 | tf_op jit(solution)/shard_map/reshape | solution.py:66
  122.5 5.7 %collective-permute-start.1 = (bf16[2,6,6,384]{3,0,2,1:T(2,128)(2,1)S(1)}, bf16[2,6,6,384]{3,0,2,1:T(2,128)(2,1)S(1)}, u32[]{:S(2)}, u32[]{:S(2)}) collective-permute-start(bf16[2,6,6,384]{3,0,2,1:T(2,128)(2,1)S(1)} %get-tuple-element.41), channel_id=1, source_target_pairs={{0,15},{1,0},{2,1},{3,2},{4,3},{5,4},{6,5},{7,6},{8,7},{9,8},{10,9... | collective-permute-start | bytes 165896 | tf_op jit(solution)/shard_map/ppermute | solution.py:10
  128.2 1.6 fusion.26
  132.7 2.0 add_select_fusion
  134.6 1.6 fusion.46
  139.1 1.6 reshape_reshape_transpose_reshape.4
  140.7 1.9 convolution_convert_fusion.2
  142.6 1.7 copy.64
  144.3 2.1 convolution_bitcast_fusion.2
  146.5 2.7 fusion.10
  149.2 3.3 convolution_bitcast_fusion.3
  152.5 3.3 convolution_bitcast_fusion.4
  155.8 3.6 subtract_multiply_fusion
  160.8 10.3 %reshape.393 = f32[12,2,6,12,2,6,12]{3,2,1,6,5,4,0:T(8,128)} reshape(f32[12,144,144]{1,2,0:T(8,128)} %subtract_multiply_fusion) | data formatting | bytes 1990656 | tf_op jit(solution)/shard_map/reshape.46
  171.1 20.8 %copy.70 = f32[12,2,6,12,2,6,12]{6,0,3,5,4,2,1:T(8,128)} copy(f32[12,2,6,12,2,6,12]{3,2,1,6,5,4,0:T(8,128)} %reshape.393) | data formatting | bytes 1990656 | tf_op jit(solution)/shard_map/reshape.46
  191.9 21.2 %convolution_bitcast_fusion.1 = f32[1,12,2,2,6,6,23]{6,1,5,3,4,2,0:T(8,128)S(1)} fusion(f32[23,12,12,1,1,1,1]{0,2,1,6,5,4,3:T(8,128)S(1)} %copy-done.16, f32[12,2,6,12,2,6,12]{6,0,3,5,4,2,1:T(8,128)} %copy.70), kind=kOutput, calls=%fused_computation.11 | convolution fusion | flops 68677632 | bytes 1167552 | tf_op jit(solution)/shard_map/whacebdf,oef->whabcdo/dot_general | solution.py:91
  215.2 1.8 fusion.47
  217.0 2.8 broadcast_multiply_fusion
  222.9 76.6 %psum.28 = f32[384]{0:T(512)} all-reduce(f32[384]{0:T(512)S(1)} %get-tuple-element.18), channel_id=1, replica_groups=mesh['lat'=16,'lon'=16] {'lat','lon'}, use_global_device_ids=true, to_apply=%region_8.9 | all-reduce | flops 384 | bytes 3072 | tf_op jit(solution)/shard_map/psum | solution.py:177
  299.6 1.8 collective-permute-start.3
  304.5 188.0 %all-reduce.3.cloned.1.call-done = (f32[384,1152]{1,0:T(8,128)}, f32[384,384]{1,0:T(8,128)}, f32[32,12,3312]{2,0,1:T(8,128)}) async-done(((f32[384,1152]{1,0:T(8,128)}, f32[384,384]{1,0:T(8,128)}, f32[32,12,3312]{2,0,1:T(8,128)}), (f32[384,1152]{1,0:T(8,128)}, f32[384,384]{1,0:T(8,128)}, f32[32,12,3312]{2,0,1:T(8,128)})) %all-reduce.3.cloned.1.call-update) | async-done | bytes 7446544 | tf_op jit(solution)/shard_map/psum | solution.py:177
  492.4 1.4 dynamic_slice.13
  495.3 1.7 constant_dynamic-slice_fusion
  (108 shorter events, 23.3 us)
Async XLA Ops:
  7.2 124.8 %copy-start = (bf16[384,1152]{1,0:T(8,128)(2,1)S(1)}, bf16[384,1152]{1,0:T(8,128)(2,1)}, u32[]{:S(2)}) copy-start(bf16[384,1152]{1,0:T(8,128)(2,1)} %param.12) | copy-start | bytes 2654212
  7.2 485.2 %all-reduce.3.cloned.1.call-start = ((), (), s32[]{:S(2)}) async-start(), calls=%async_computation | async-start | bytes 14942208 | tf_op jit(solution)/shard_map/psum | solution.py:177
  9.3 111.7 %collective-permute-start = (bf16[2,3,12,384]{3,0,2,1:T(2,128)(2,1)S(1)}, bf16[2,3,12,384]{3,0,2,1:T(2,128)(2,1)S(1)}, u32[]{:S(2)}, u32[]{:S(2)}) collective-permute-start(bf16[2,3,12,384]{3,0,2,1:T(2,128)(2,1)S(1)} %get-tuple-element.27), channel_id=1, source_target_pairs={{0,240},{16,0},{32,16},{48,32},{64,48},{80,64},{96,80},{112,96},{1... | collective-permute-start | bytes 165896 | tf_op jit(solution)/shard_map/ppermute | solution.py:10
  14.6 113.6 %collective-permute-start.4 = (bf16[2,3,12,384]{3,0,2,1:T(2,128)(2,1)}, bf16[2,3,12,384]{3,0,2,1:T(2,128)(2,1)}, u32[]{:S(2)}, u32[]{:S(2)}) collective-permute-start(bf16[2,3,12,384]{3,0,2,1:T(2,128)(2,1)} %get-tuple-element.25), channel_id=1, source_target_pairs={{0,240},{16,0},{32,16},{48,32},{64,48},{80,64},{96,80},{112,96},{1... | collective-permute-start | bytes 165896 | tf_op jit(solution)/shard_map/ppermute | solution.py:10
  36.0 17.0 %copy-start.19 = (s32[2,6,12]{2,0,1:T(2,128)S(1)}, s32[2,6,12]{2,0,1:T(2,128)}, u32[]{:S(2)}) copy-start(s32[2,6,12]{2,0,1:T(2,128)} %param.16) | copy-start | bytes 1732
  53.8 21.4 %copy-start.15 = (f32[23,12,12,1,1,1,1]{0,2,6,5,4,3,1:T(8,128)S(1)}, f32[23,12,12,1,1,1,1]{0,2,6,5,4,3,1:T(8,128)}, u32[]{:S(2)}) copy-start(f32[23,12,12,1,1,1,1]{0,2,6,5,4,3,1:T(8,128)} %constant.100) | copy-start | bytes 39748
  110.7 10.9 %copy-start.12 = (bf16[2,3,12,384]{3,0,2,1:T(2,128)(2,1)S(1)}, bf16[2,3,12,384]{3,0,2,1:T(2,128)(2,1)}, u32[]{:S(2)}) copy-start(bf16[2,3,12,384]{3,0,2,1:T(2,128)(2,1)} %get-tuple-element.26) | copy-start | bytes 165892
  110.7 17.5 %copy-start.11 = (bf16[2,3,12,384]{3,0,2,1:T(2,128)(2,1)S(1)}, bf16[2,3,12,384]{3,0,2,1:T(2,128)(2,1)}, u32[]{:S(2)}) copy-start(bf16[2,3,12,384]{3,0,2,1:T(2,128)(2,1)} %get-tuple-element.24) | copy-start | bytes 165892
  121.0 11.0 %copy-start.18 = (f32[384]{0:T(512)S(1)}, f32[384]{0:T(512)}, u32[]{:S(2)}) copy-start(f32[384]{0:T(512)} %param.11) | copy-start | bytes 4612
  121.0 0.6 copy-start.17
  122.5 8.0 %collective-permute-start.1 = (bf16[2,6,6,384]{3,0,2,1:T(2,128)(2,1)S(1)}, bf16[2,6,6,384]{3,0,2,1:T(2,128)(2,1)S(1)}, u32[]{:S(2)}, u32[]{:S(2)}) collective-permute-start(bf16[2,6,6,384]{3,0,2,1:T(2,128)(2,1)S(1)} %get-tuple-element.41), channel_id=1, source_target_pairs={{0,15},{1,0},{2,1},{3,2},{4,3},{5,4},{6,5},{7,6},{8,7},{9,8},{10,9... | collective-permute-start | bytes 165896 | tf_op jit(solution)/shard_map/ppermute | solution.py:10
  129.8 7.7 %collective-permute-start.5 = (bf16[2,6,6,384]{3,0,2,1:T(2,128)(2,1)}, bf16[2,6,6,384]{3,0,2,1:T(2,128)(2,1)}, u32[]{:S(2)}, u32[]{:S(2)}) collective-permute-start(bf16[2,6,6,384]{3,0,2,1:T(2,128)(2,1)} %get-tuple-element.37), channel_id=1, source_target_pairs={{0,15},{1,0},{2,1},{3,2},{4,3},{5,4},{6,5},{7,6},{8,7},{9,8},{10,9... | collective-permute-start | bytes 165896 | tf_op jit(solution)/shard_map/ppermute | solution.py:10
  130.5 1.2 copy-start.4
  130.9 0.8 copy-start.7
  131.4 0.6 copy-start.9
  146.5 2.7 copy-start.1
  155.8 3.7 copy-start.5
  155.8 3.7 copy-start.8
  155.8 3.7 copy-start.10
  155.8 4.0 copy-start.2
  155.8 4.0 copy-start.6
  171.1 20.8 %copy-start.16 = (f32[23,12,12,1,1,1,1]{0,2,1,6,5,4,3:T(8,128)S(1)}, f32[23,12,12,1,1,1,1]{0,2,1,6,5,4,3:T(8,128)}, u32[]{:S(2)}) copy-start(f32[23,12,12,1,1,1,1]{0,2,1,6,5,4,3:T(8,128)} %constant.101) | copy-start | bytes 39748
  213.1 0.9 copy-start.13
  213.1 1.0 copy-start.14
  219.8 1.0 copy-start.3
  221.1 78.4 %collective-permute-start.2 = (bf16[2,6,6,384]{3,2,1,0:T(8,128)(2,1)S(1)}, bf16[2,6,6,384]{3,2,1,0:T(8,128)(2,1)S(1)}, u32[]{:S(2)}, u32[]{:S(2)}) collective-permute-start(bf16[2,6,6,384]{3,2,1,0:T(8,128)(2,1)S(1)} %get-tuple-element.34), channel_id=1, source_target_pairs={{0,1},{1,2},{2,3},{3,4},{4,5},{5,6},{6,7},{7,8},{8,9},{9,10},{10,1... | collective-permute-start | bytes 165896 | tf_op jit(solution)/shard_map/ppermute | solution.py:10
  222.8 78.5 %collective-permute-start.6 = (bf16[2,6,6,384]{3,2,1,0:T(8,128)(2,1)S(1)}, bf16[2,6,6,384]{3,2,1,0:T(8,128)(2,1)S(1)}, u32[]{:S(2)}, u32[]{:S(2)}) collective-permute-start(bf16[2,6,6,384]{3,2,1,0:T(8,128)(2,1)S(1)} %get-tuple-element.30), channel_id=1, source_target_pairs={{0,1},{1,2},{2,3},{3,4},{4,5},{5,6},{6,7},{7,8},{8,9},{9,10},{10,1... | collective-permute-start | bytes 165896 | tf_op jit(solution)/shard_map/ppermute | solution.py:10
  299.6 3.2 collective-permute-start.3
  301.4 2.2 collective-permute-start.7
Sparse Core Ops, SparseCore 0:
  220.0 272.4 all-reduce.2
where the time goes:
time: 510 us; the launch traced here: 504 us
  waiting for transfers between devices  189 us (37%)
  local copies, waits for them, and re-layouts  113 us (22%)
  matrix products  77.2 us (15%)
  blocking collectives  76.6 us (15%)
  other arithmetic  16.3 us (3%)
  starting transfers between devices  16.2 us (3%)
  between operations  15.3 us (3%)
    psum x1, waiting for transfers between devices, local(): lax.psum((grad_bias, grad_qkv, grad_proj, grad_gain), ('lat', 'lon'))  188 us
    psum x1, blocking collectives, local(): lax.psum((grad_bias, grad_qkv, grad_proj, grad_gain), ('lat', 'lon'))  76.6 us
    another operation x4, local copies, waits for them, and re-layouts  47.8 us
    reshape x2, local copies, waits for them, and re-layouts, window_pass(): bias_full = bias_full.reshape(win_count, head_count, tokens_win, tokens_win)  31.9 us
    dot_general x1, matrix products, local(): jnp.dot(onehot, bias_table.reshape(type_count, -1), preferred_element_typ...  21.4 us
    dot_general x1, matrix products, window_pass(): jnp.einsum('whacebdf,oef->whabcdo', score_parts, spread_table, precision=...  21.2 us
    ppermute x8, starting transfers between devices, from_behind(): lax.ppermute(value, axis, [(i, (i + by) % devices) for i in range(devices)])  16.2 us
    dot_general x6, matrix products, product(): jnp.einsum(pattern, left_op, right_op, preferred_element_type=jnp.float32)  14.6 us
  transfers between devices with their start and end apart: 9, of which 2 were waited for; matrix products, arithmetic and copies ran while one was open for 23% of the time, Pallas kernels for 0%

commit v1 on v0

v1 whole, which is shorter than its diff:
```python
import functools

import jax
import jax.numpy as jnp
import numpy as np
from jax import lax
from jax.experimental import pallas as pl
from jax.experimental.pallas import tpu as pltpu
from jax.sharding import PartitionSpec as P

F32 = jnp.float32
BF16 = jnp.bfloat16
MESH = pl.DeviceIdType.MESH
SCALE = 32 ** (-0.5)


def patterns():
    pack = np.zeros((320, 384), np.float32)
    order = np.zeros((288, 320), np.float32)
    toeplitz = np.zeros((6, 1024, 144), np.float32)
    dup = np.zeros((2, 288, 192), np.float32)
    key_rows = np.zeros((144, 16), np.float32)
    key_cols = np.zeros((144, 128), np.float32)
    halves = np.zeros((384, 512), np.float32)
    for l in range(2):
        for r in range(6):
            for c in range(12):
                p = 12 * c + 6 * l + r
                quad = 2 * (r // 3) + c // 6
                t = (l * 3 + r % 3) * 6 + c % 6
                slab = 16 * (6 * l + r) + c
                pack[80 * quad + t, slab] = 1
                pack[80 * quad + 36 + t, 192 + slab] = 1
                order[p, 80 * quad + t] = 1
                order[144 + p, 80 * quad + 36 + t] = 1
                key_rows[p, 8 * (1 - l) + (r + 3) % 6] = 1
                key_cols[p, (c + 6) % 12] = 1
                for m in range(6):
                    for par in range(2):
                        spot = (2 * m + par + 6) % 12 - (c + 6) % 12 + 11
                        iq = (r + 3) % 6
                        lane = ((1 - l) * 2 + iq // 3) * 128 + (iq % 3) * 23 + spot
                        toeplitz[m, 512 * par + lane, p] = 1
    for h in range(12):
        for par in range(2):
            for l in range(2):
                for r in range(6):
                    zi = (1 - l) * 6 + (r + 3) % 6
                    dup[par, 24 * h + 12 * par + 6 * l + r, 16 * zi + h] = 1
    for f in range(384):
        i = f // 24
        halves[f, 256 * (i % 2) + 24 * (i // 2) + f % 24] = 1
    both = [
        pack,
        pack.T,
        order,
        order.T,
        toeplitz,
        dup,
        dup.transpose(0, 2, 1),
        key_rows,
        key_cols,
        key_cols.T,
        halves,
    ]
    return [jnp.asarray(x, BF16) for x in both]


def dot(a, b, ca=1, cb=0):
    return lax.dot_general(a, b, (((ca,), (cb,)), ((), ())), preferred_element_type=F32)


def roll_left(value, by):
    width = value.shape[1]
    by = by % width
    return value if by == 0 else pltpu.roll(value, width - by, 1)


def kernel(
    in_ref,
    cot_ref,
    gain_ref,
    wqkv_hbm,
    wproj_hbm,
    table_hbm,
    type_ref,
    region_ref,
    *rest,
):
    const_hbm = rest[:11]
    out_ref, gin_ref, ggain_ref, gqkv_ref, gproj_ref, gbias_ref = rest[11:17]
    wqkv, wproj, table = rest[17:20]
    const = rest[20:31]
    (
        slabs, qs, qr, rs, rr, keys, trow, amat, bias, gsb, gj, att,
        hs_own, hs_out, hs_in, as_own, as_out, as_in, gj_in, cw, cw_in,
        ysend, yrecv, xsend, xrecv, lsend, lrecv, bsend, brecv, asend, arecv,
        load_sem, halo_s, halo_r, back_s, back_r, sib_s, sib_r, y_s, y_r, x_s, x_r,
        l_s, l_r, b_s, b_r, a_s, a_r,
    ) = rest[31:]
    pack, pack_t, order, order_t, toep, dup, dup_t, key_rows, key_cols, key_cols_t, halves = const

    i = lax.axis_index("lat")
    j = lax.axis_index("lon")
    y, x, core = i // 4, (i // 2) % 2, i % 2
    sibling = (i + 1 - 2 * core, j)
    up, down = (i + 15) % 16, (i + 1) % 16
    left, right = (j + 15) % 16, (j + 1) % 16

    def remote(src, dst, ssem, rsem, dev):
        return pltpu.make_async_remote_copy(
            src_ref=src, dst_ref=dst, send_sem=ssem, recv_sem=rsem,
            device_id=dev, device_id_type=MESH,
        )

    loads = [
        pltpu.make_async_copy(s, d, load_sem.at[n])
        for n, (s, d) in enumerate(
            zip(
                (*const_hbm, wqkv_hbm, wproj_hbm, table_hbm),
                (*const, wqkv, wproj, table),
            )
        )
    ]
    for c in loads:
        c.start()

    barrier = pltpu.get_barrier_semaphore()

    def greet(d, carry):
        pl.semaphore_signal(barrier, inc=1, device_id=((i + d) % 16, j), device_id_type=MESH)
        pl.semaphore_signal(barrier, inc=1, device_id=(i, (j + d) % 16), device_id_type=MESH)
        return carry

    lax.fori_loop(1, 16, greet, 0)
    pl.semaphore_signal(barrier, inc=1, device_id=(up, left), device_id_type=MESH)
    pl.semaphore_signal(barrier, inc=1, device_id=(down, right), device_id_type=MESH)

    slabs[...] = jnp.zeros((384, 384), BF16)
    for l in range(2):
        for r in range(6):
            s = 16 * (6 * l + r)
            slabs[s : s + 12, :] = in_ref[l, r]
            slabs[192 + s : 192 + s + 12, :] = cot_ref[l, r]
    loads[0].wait()
    packed = dot(pack[...], slabs[...]).astype(BF16)
    for k in range(4):
        qs[k] = packed[80 * k : 80 * k + 80]
    pl.semaphore_wait(barrier, 32)
    halo = [
        remote(qs.at[k], qr.at[k], halo_s.at[k], halo_r.at[k], dev)
        for k, dev in enumerate(((up, left), (up, j), (i, left)))
    ]
    for c in halo:
        c.start()

    for n in range(1, 11):
        loads[n].wait()
    row_id = lax.broadcasted_iota(jnp.int32, (6, 12), 0)
    lat_side = (6 * i + row_id + 3 >= 96).astype(jnp.int32) * 2
    keys[...] = jnp.zeros((16, 128), F32)
    keys[0:6, 0:12] = (region_ref[0] * 4 + lat_side).astype(F32)
    keys[8:14, 0:12] = (region_ref[1] * 4 + lat_side + 1).astype(F32)
    key_grid = keys[...].astype(BF16)
    key_p = jnp.sum(
        dot(key_rows[...], key_grid) * key_cols[...].astype(F32), 1, keepdims=True
    )
    key_q = jnp.sum(
        dot(key_grid, key_rows[...], 0, 1) * key_cols_t[...].astype(F32), 0, keepdims=True
    )
    allowed = key_p == key_q

    loads[13].wait()
    kind = type_ref[0, 0]
    trow[...] = jnp.zeros((16, 3456), F32)
    trow[0:12, 0:3312] = table[kind].astype(F32)
    for zp in range(2):
        for ip in range(6):
            for b in range(4):
                off = ((2 * zp + b // 2) * 36 + 6 * ip + 3 * (b % 2)) * 23
                a = off // 128 * 128
                piece = roll_left(trow[:, a : a + 256], off - a)[:, :128]
                row = (6 * zp + ip) * 16
                amat[row : row + 16, 128 * b : 128 * b + 128] = piece.astype(BF16)
    spread0 = dot(dup[0], amat[...]).astype(BF16)
    spread1 = dot(dup[1], amat[...]).astype(BF16)
    for m in range(6):
        part = dot(spread0, toep[m, 0:512]) + dot(spread1, toep[m, 512:1024])
        ok = allowed[24 * m : 24 * m + 24]
        for h in range(12):
            bias[h, 24 * m : 24 * m + 24, :] = jnp.where(ok, part[24 * h : 24 * h + 24], -1e30)
    loads[11].wait()
    loads[12].wait()

    for c in halo:
        c.wait_recv()
    tokens = jnp.concatenate([qr[0], qr[1], qr[2], qs[3]], 0)
    both = dot(order[...], tokens)
    wide = both[0:144]
    cw[...] = both[144:288].astype(BF16)
    to_sib = [
        remote(cw, cw_in, sib_s.at[0], sib_r.at[0], sibling),
        remote(hs_out, hs_in, sib_s.at[1], sib_r.at[1], sibling),
        remote(as_out, as_in, sib_s.at[2], sib_r.at[2], sibling),
        remote(gj, gj_in, sib_s.at[3], sib_r.at[3], sibling),
    ]
    to_sib[0].start()

    def split_halves(value, own, out):
        spread = dot(value, halves[...]).astype(BF16)
        first, second = spread[:, 0:256], spread[:, 256:512]
        own[...] = jnp.where(core == 0, first, second)
        out[...] = jnp.where(core == 0, second, first)

    gain = gain_ref[...]
    center = jnp.mean(wide, 1, keepdims=True)
    shifted = wide - center
    inv_std = lax.rsqrt(jnp.mean(jnp.square(shifted), 1, keepdims=True) + 1e-05)
    normed = shifted * inv_std
    hidden = (normed * gain).astype(BF16)
    joined = dot(hidden, wqkv[...]).astype(BF16)
    split_halves(hidden, hs_own, hs_out)
    to_sib[1].start()
    cot_rows = cw[...]
    grad_att = dot(cot_rows, wproj[...], 1, 1).astype(BF16)

    lane_head = lax.broadcasted_iota(jnp.int32, (1, 128), 1) // 32
    head_masks = [(lane_head == h).astype(F32).astype(BF16) for h in range(4)]
    wide_masks = [(lane_head == h).astype(F32) for h in range(4)]

    def pick(stacked):
        total = stacked[0:144] * wide_masks[0]
        for h in range(1, 4):
            total = total + stacked[144 * h : 144 * h + 144] * wide_masks[h]
        return total

    for g in range(3):
        lanes = slice(128 * g, 128 * g + 128)
        queries = joined[:, 128 * g : 128 * g + 128]
        key_part = joined[:, 384 + 128 * g : 384 + 128 * g + 128]
        value_part = joined[:, 768 + 128 * g : 768 + 128 * g + 128]
        grad_part = grad_att[:, lanes]
        queries4 = jnp.concatenate([queries * k for k in head_masks], 0)
        grad4 = jnp.concatenate([grad_part * k for k in head_masks], 0)
        scores = dot(queries4, key_part, 1, 1) * SCALE
        scores = scores + bias[4 * g : 4 * g + 4].reshape(576, 144)
        top = jnp.max(scores, 1, keepdims=True)
        probs = jnp.exp(scores - top)
        probs = probs * (1.0 / jnp.sum(probs, 1, keepdims=True))
        probs_low = probs.astype(BF16)
        att[:, lanes] = pick(dot(probs_low, value_part)).astype(BF16)
        grad_probs = dot(grad4, value_part, 1, 1)
        grad_values = dot(probs_low, grad4, 0, 0)
        grad_scores = probs * (grad_probs - jnp.sum(probs * grad_probs, 1, keepdims=True))
        for h in range(4):
            for m in range(6):
                row = 24 * (4 * g + h)
                gsb[m, row : row + 24, :] = grad_scores[144 * h + 24 * m : 144 * h + 24 * m + 24]
        grad_scaled = (grad_scores * SCALE).astype(BF16)
        grad_query = pick(dot(grad_scaled, key_part))
        grad_keys = dot(grad_scaled, queries4, 0, 0)
        gj[:, 128 * g : 128 * g + 128] = grad_query.astype(BF16)
        gj[:, 384 + 128 * g : 384 + 128 * g + 128] = grad_keys.astype(BF16)
        gj[:, 768 + 128 * g : 768 + 128 * g + 128] = grad_values.astype(BF16)
    to_sib[3].start()
    attended = att[...]
    split_halves(attended, as_own, as_out)
    to_sib[2].start()

    result = (wide + dot(attended, wproj[...])).astype(BF16)
    grad_hidden = dot(gj[...], wqkv[...], 1, 1)
    grad_gain = jnp.sum(grad_hidden * normed, 0, keepdims=True)
    grad_normed = grad_hidden * gain
    grad_wide = inv_std * (
        grad_normed
        - jnp.mean(grad_normed, 1, keepdims=True)
        - normed * jnp.mean(grad_normed * normed, 1, keepdims=True)
    )
    grad_in = (cot_rows.astype(F32) + grad_wide).astype(BF16)
    returned = dot(order_t[...], jnp.concatenate([result, grad_in], 0)).astype(BF16)
    for k in range(4):
        rs[k] = returned[80 * k : 80 * k + 80]
    back = [
        remote(rs.at[k], rr.at[k], back_s.at[k], back_r.at[k], dev)
        for k, dev in enumerate(((down, right), (down, j), (i, right)))
    ]
    for c in back:
        c.start()

    folded = dot(gsb[0].astype(BF16), toep[0], 1, 1)
    for m in range(1, 6):
        folded = folded + dot(gsb[m].astype(BF16), toep[m], 1, 1)
    folded = folded.astype(BF16)
    shares = dot(dup_t[0], folded[:, 0:512]) + dot(dup_t[1], folded[:, 512:1024])
    block_row = lax.broadcasted_iota(jnp.int32, (16, 128), 0)

    def riders(gain_row, kind_row):
        high = gain_row.astype(BF16).astype(F32)
        low = gain_row - high
        return [
            jnp.where(block_row == 12, high[:, 128 * b : 128 * b + 128], 0.0)
            + jnp.where(block_row == 13, low[:, 128 * b : 128 * b + 128], 0.0)
            + jnp.where(block_row == 14, kind_row, 0.0)
            for b in range(3)
        ]

    extra = riders(grad_gain, kind.astype(F32))
    for dest in range(16):
        zp, zq, k = dest // 8, (dest // 4) % 2, dest % 4
        for b in range(3):
            ip, iqh = (3 * k + b) // 2, (3 * k + b) % 2
            row, lane = (6 * zp + ip) * 16, (2 * zq + iqh) * 128
            block = shares[row : row + 16, lane : lane + 128] + extra[b]
            bsend[dest, :, 128 * b : 128 * b + 128] = block.astype(BF16)

    def bias_lon(d):
        to = (j + d) % 16
        return remote(bsend.at[to], brecv.at[d], b_s.at[d], b_r.at[d], (i, to))

    def start_all(make):
        def body(d, carry):
            make(d).start()
            return carry

        lax.fori_loop(1, 16, body, 0)

    def wait_all(make):
        def body(d, carry):
            make(d).wait_recv()
            return carry

        lax.fori_loop(1, 16, body, 0)

    def sent_all(make):
        def body(d, carry):
            make(d).wait_send()
            return carry

        lax.fori_loop(1, 16, body, 0)

    start_all(bias_lon)

    for c in to_sib:
        c.wait_recv()
    g_qkv = dot(hs_own[...], gj[...], 0, 0) + dot(hs_in[...], gj_in[...], 0, 0)
    g_proj = dot(as_own[...], cw[...], 0, 0) + dot(as_in[...], cw_in[...], 0, 0)
    for k in range(4):
        ysend[k, :, 0:1152] = g_qkv[48 * k : 48 * k + 48].astype(BF16)
        ysend[k, :, 1152:1536] = g_proj[48 * k : 48 * k + 48].astype(BF16)

    def to_y(d):
        k = (y + d) % 4
        return remote(
            ysend.at[k], yrecv.at[d], y_s.at[d], y_r.at[d], (4 * k + 2 * x + core, j)
        )

    y_copies = [to_y(d) for d in range(1, 4)]
    for c in y_copies:
        c.start()

    wait_all(bias_lon)
    total = bsend[j].astype(F32)
    for d in range(1, 16):
        total = total + brecv[d].astype(F32)
    gain_lon = total[12:13] + total[13:14]
    kinds = total[14:15, 0:1] * (1.0 / 16.0)
    extra = riders(gain_lon, kinds)
    for b in range(3):
        lanes = slice(128 * b, 128 * b + 128)
        block = jnp.where(block_row < 12, total[:, lanes], 0.0) + extra[b]
        asend[:, lanes] = block.astype(BF16)

    def bias_lat(d):
        return remote(asend, arecv.at[d], a_s.at[d], a_r.at[d], ((i + d) % 16, j))

    start_all(bias_lat)

    for c in back:
        c.wait_recv()
    tokens = jnp.concatenate([rr[0], rr[1], rr[2], rs[3]], 0)
    final = dot(pack_t[...], tokens).astype(BF16)
    for l in range(2):
        for r in range(6):
            s = 16 * (6 * l + r)
            out_ref[l, r] = final[s : s + 12]
            gin_ref[l, r] = final[192 + s : 192 + s + 12]

    for c in y_copies:
        c.wait_recv()
    chunk = ysend[y].astype(F32)
    for d in range(1, 4):
        chunk = chunk + yrecv[d].astype(F32)
    mine = jnp.where(x == 0, chunk[0:24], chunk[24:48])
    other = jnp.where(x == 0, chunk[24:48], chunk[0:24])
    xsend[...] = jnp.concatenate([other[:, 0:768], other[:, 768:1536]], 0).astype(BF16)
    to_x = remote(xsend, xrecv, x_s, x_r, (4 * y + 2 * (1 - x) + core, j))
    to_x.start()

    wait_all(bias_lat)
    gain_total = jnp.zeros((1, 384), F32)
    sums = [jnp.zeros((16, 384), F32), jnp.zeros((16, 384), F32)]
    for d in range(16):
        block = asend[...] if d == 0 else arecv[d]
        block = block.astype(F32)
        gain_total = gain_total + block[12:13] + block[13:14]
        kind_row = block[14:15]
        for t in range(2):
            hit = kind_row == (2 * i + t).astype(F32)
            sums[t] = sums[t] + jnp.where(hit, block, 0.0)
    ggain_ref[...] = gain_total
    lane256 = lax.broadcasted_iota(jnp.int32, (16, 256), 1)
    for t in range(2):
        parts = [
            pltpu.roll(
                jnp.concatenate(
                    [sums[t][:, 128 * b : 128 * b + 128], jnp.zeros((16, 128), F32)], 1
                ),
                69 * b,
                1,
            )
            if b
            else jnp.concatenate([sums[t][:, 0:128], jnp.zeros((16, 128), F32)], 1)
            for b in range(3)
        ]
        row = jnp.where(lane256 < 69, parts[0], jnp.where(lane256 < 138, parts[1], parts[2]))
        gbias_ref[t] = row[0:12, 0:207]

    to_x.wait_recv()
    got = xrecv[...].astype(F32)
    mine = mine + jnp.concatenate([got[0:24], got[24:48]], 1)
    lane128 = lax.broadcasted_iota(jnp.int32, (24, 128), 1)
    for dest in range(16):
        off = 72 * dest
        a = min(off // 128 * 128, 896)
        piece = roll_left(mine[:, a : a + 256], off - a)[:, :128]
        off = 24 * dest
        a = min(off // 128 * 128, 128)
        tail = roll_left(mine[:, 1152 + a : 1152 + a + 256], off - a - 72)[:, :128]
        block = jnp.where(lane128 < 72, piece, tail)
        block = jnp.concatenate([block, jnp.zeros((8, 128), F32)], 0)
        lsend[dest] = block.astype(BF16)

    def to_lon(d):
        to = (j + d) % 16
        return remote(lsend.at[to], lrecv.at[d], l_s.at[d], l_r.at[d], (i, to))

    start_all(to_lon)
    for c in (*halo, *to_sib, *back, *y_copies, to_x):
        c.wait_send()
    sent_all(bias_lon)
    sent_all(bias_lat)
    wait_all(to_lon)
    total = lsend[j].astype(F32)
    for d in range(1, 16):
        total = total + lrecv[d].astype(F32)
    gqkv_ref[...] = total[0:24, 0:72]
    gproj_ref[...] = roll_left(total[0:24], 72)[:, 0:24]
    sent_all(to_lon)


def local(inputs, cotangent, norm_gain, qkv_weight, proj_weight, bias_table, window_type, region):
    consts = patterns()
    vmem = pl.BlockSpec(memory_space=pltpu.VMEM)
    anywhere = pl.BlockSpec(memory_space=pl.ANY)
    dma = pltpu.SemaphoreType.DMA
    tokens = (2, 6, 12, 384)
    outs = pl.pallas_call(
        kernel,
        out_shape=[
            jax.ShapeDtypeStruct(tokens, BF16),
            jax.ShapeDtypeStruct(tokens, BF16),
            jax.ShapeDtypeStruct((1, 384), F32),
            jax.ShapeDtypeStruct((24, 72), F32),
            jax.ShapeDtypeStruct((24, 24), F32),
            jax.ShapeDtypeStruct((2, 12, 207), F32),
        ],
        in_specs=[vmem, vmem, vmem, anywhere, anywhere, anywhere]
        + [pl.BlockSpec(memory_space=pltpu.SMEM), vmem]
        + [anywhere] * len(consts),
        out_specs=[vmem] * 6,
        scratch_shapes=[
            pltpu.VMEM(qkv_weight.shape, BF16),
            pltpu.VMEM(proj_weight.shape, BF16),
            pltpu.VMEM(bias_table.shape, BF16),
        ]
        + [pltpu.VMEM(c.shape, BF16) for c in consts]
        + [
            pltpu.VMEM((384, 384), BF16),
            pltpu.VMEM((4, 80, 384), BF16),
            pltpu.VMEM((3, 80, 384), BF16),
            pltpu.VMEM((4, 80, 384), BF16),
            pltpu.VMEM((3, 80, 384), BF16),
            pltpu.VMEM((16, 128), F32),
            pltpu.VMEM((16, 3456), F32),
            pltpu.VMEM((192, 512), BF16),
            pltpu.VMEM((12, 144, 144), F32),
            pltpu.VMEM((6, 288, 144), F32),
            pltpu.VMEM((144, 1152), BF16),
            pltpu.VMEM((144, 384), BF16),
            pltpu.VMEM((144, 256), BF16),
            pltpu.VMEM((144, 256), BF16),
            pltpu.VMEM((144, 256), BF16),
            pltpu.VMEM((144, 256), BF16),
            pltpu.VMEM((144, 256), BF16),
            pltpu.VMEM((144, 256), BF16),
            pltpu.VMEM((144, 1152), BF16),
            pltpu.VMEM((144, 384), BF16),
            pltpu.VMEM((144, 384), BF16),
            pltpu.VMEM((4, 48, 1536), BF16),
            pltpu.VMEM((4, 48, 1536), BF16),
            pltpu.VMEM((48, 768), BF16),
            pltpu.VMEM((48, 768), BF16),
            pltpu.VMEM((16, 32, 128), BF16),
            pltpu.VMEM((16, 32, 128), BF16),
            pltpu.VMEM((16, 16, 384), BF16),
            pltpu.VMEM((16, 16, 384), BF16),
            pltpu.VMEM((16, 384), BF16),
            pltpu.VMEM((16, 16, 384), BF16),
            dma((len(consts) + 3,)),
            dma((3,)), dma((3,)), dma((3,)), dma((3,)), dma((4,)), dma((4,)),
            dma((4,)), dma((4,)), dma, dma,
            dma((16,)), dma((16,)), dma((16,)), dma((16,)), dma((16,)), dma((16,)),
        ],
        compiler_params=pltpu.CompilerParams(
            collective_id=0, has_side_effects=True, vmem_limit_bytes=48 * 2**20
        ),
    )(
        inputs,
        cotangent,
        norm_gain.reshape(1, -1),
        qkv_weight,
        proj_weight,
        bias_table,
        window_type,
        region,
        *consts,
    )
    block_out, grad_inputs, grad_gain, grad_qkv, grad_proj, grad_bias = outs
    return block_out, grad_inputs, grad_gain.reshape(-1), grad_qkv, grad_proj, grad_bias


def solution(mesh):
    return jax.shard_map(
        local,
        mesh=mesh,
        in_specs=(
            P(None, "lat", "lon", None),
            P(None, "lat", "lon", None),
            P(),
            P(),
            P(),
            P(),
            P("lat", None),
            P(None, "lat", "lon"),
        ),
        out_specs=(
            P(None, "lat", "lon", None),
            P(None, "lat", "lon", None),
            P(),
            P("lat", "lon"),
            P("lat", "lon"),
            P("lat", None, "lon"),
        ),
        check_vma=False,
    )
```

time: 510 us -> 60.4 us (0.12); the launches traced: 504 us -> 60.2 us
  waiting for transfers between devices: 189 us -> 0 us
  local copies, waits for them, and re-layouts: 113 us -> 11.6 us
  matrix products: 77.2 us -> 0 us
  blocking collectives: 76.6 us -> 0 us
  Pallas kernels: 0 us -> 46.5 us
  starting transfers between devices: 16.2 us -> 0 us
  other arithmetic: 16.3 us -> 0.6 us
  between operations: 15.3 us -> 1.47 us
    psum x1 -> x0, waiting for transfers between devices: 188 us -> none  [local(): lax.psum((grad_bias, grad_qkv, grad_proj, grad_gain), ('lat', 'lon'))]
    dot_general x15 -> x0, matrix products: 77.2 us -> none  [the longest x1 21.4 us: local(): jnp.dot(onehot, bias_table.reshape(type_count, -1), preferred_element_typ...]
    psum x1 -> x0, blocking collectives: 76.6 us -> none  [local(): lax.psum((grad_bias, grad_qkv, grad_proj, grad_gain), ('lat', 'lon'))]
    another operation x7 -> x0, local copies, waits for them, and re-layouts: 49.5 us -> none
    pallas_call x0 -> x1, Pallas kernels: none -> 46.5 us  [local(): pl.pallas_call(kernel, out_shape=[jax.ShapeDtypeStruct(tokens, BF16), jax...]
    reshape x3 -> x1, local copies, waits for them, and re-layouts: 37.5 us -> 0.68 us  [local(): norm_gain.reshape(1, -1)]
    ppermute x8 -> x0, starting transfers between devices: 16.2 us -> none  [from_behind(): lax.ppermute(value, axis, [(i, (i + by) % devices) for i in range(devices)])]
    dot_general x1 -> x0, local copies, waits for them, and re-layouts: 7.2 us -> none  [local(): jnp.dot(onehot, bias_table.reshape(type_count, -1), preferred_element_typ...]
  transfers between devices with their start and end apart: 9 -> 0, of which waited for: 2 -> 0; matrix products, arithmetic and copies ran while one was open for 23% -> 0% of each run, Pallas kernels for 0% -> 0%
where the time goes in v1:
time: 60.4 us; the launch traced here: 60.2 us
  Pallas kernels  46.5 us (77%)
  local copies, waits for them, and re-layouts  11.6 us (19%)
  between operations  1.47 us (2%)
    pallas_call x1, Pallas kernels, local(): pl.pallas_call(kernel, out_shape=[jax.ShapeDtypeStruct(tokens, BF16), jax...  46.5 us
    unnamed x33, local copies, waits for them, and re-layouts  10.9 us

profile of v1, /device:TPU:1, one launch (start us, length us, event | category | flops | bytes accessed | tf_op | source)
XLA Modules:
  0.0 60.2 jit_solution(14316382469626278943)
XLA Ops:
  1.3 0.7 %reshape.18.gain_ref = f32[1,384]{1,0:T(1,128)S(1)} reshape(f32[384]{0:T(512)} %param.21) | data formatting | bytes 3072 | tf_op jit(solution)/shard_map/reshape | solution.py:530
  2.0 0.7 %copy.28.region_ref = s32[2,6,12]{2,1,0:T(8,128)S(1)} copy(s32[2,6,12]{2,0,1:T(2,128)} %param.26) | data formatting | bytes 1152 | tf_op args[7]
  2.7 0.9 %copy.25.in_ref = bf16[2,6,12,384]{3,2,1,0:T(8,128)(2,1)S(1)} copy(bf16[2,6,12,384]{3,0,2,1:T(2,128)(2,1)} %param.19) | data formatting | bytes 221184 | tf_op args[0]
  3.6 0.0 copy-start
  3.6 0.0 copy-start.1
  3.6 0.0 copy-start.2
  3.6 0.0 copy-start.3
  3.6 0.0 copy-start.4
  3.6 0.0 copy-start.5
  3.6 0.0 copy-start.6
  3.7 0.0 copy-start.7
  3.7 0.0 copy-start.8
  3.7 0.0 copy-start.9
  3.7 0.0 copy-start.10
  3.7 0.0 copy-start.11
  3.7 1.1 %copy.26.cot_ref = bf16[2,6,12,384]{3,2,1,0:T(8,128)(2,1)S(1)} copy(bf16[2,6,12,384]{3,0,2,1:T(2,128)(2,1)} %param.20) | data formatting | bytes 221184 | tf_op args[1]
  4.8 4.9 %copy.27.table_hbm = bf16[32,12,3312]{2,1,0:T(8,128)(2,1)} copy(bf16[32,12,3312]{2,0,1:T(8,128)(2,1)} %param.24) | data formatting | bytes 5087232 | tf_op args[5]
  9.7 0.0 copy-done
  9.7 0.0 copy-done.1
  9.7 0.0 copy-done.2
  9.7 0.0 copy-done.3
  9.7 0.0 copy-done.4
  9.7 0.0 copy-done.5
  9.7 0.0 copy-done.6
  9.7 0.0 copy-done.7
  9.8 46.5 %shard_map.226 = (bf16[2,6,12,384]{3,2,1,0:T(8,128)(2,1)S(1)}, bf16[2,6,12,384]{3,2,1,0:T(8,128)(2,1)S(1)}, f32[1,384]{1,0:T(1,128)S(1)}, f32[24,72]{1,0:T(8,128...) custom-call(bf16[2,6,12,384]{3,2,1,0:T(8,128)(2,1)S(1)} %copy.25.in_ref, ...), custom_call_target="tpu_custom_call" | custom-call | tf_op jit(solution)/shard_map/pallas_call | solution.py:467
  56.3 0.7 %copy.29 = bf16[2,6,12,384]{3,0,2,1:T(2,128)(2,1)} copy(bf16[2,6,12,384]{3,2,1,0:T(8,128)(2,1)S(1)} %get-tuple-element.18) | data formatting | bytes 221184
  57.0 0.6 reduce
  57.6 0.6 %copy.31 = f32[2,12,207]{2,0,1:T(2,128)} copy(f32[2,12,207]{2,1,0:T(8,128)S(1)} %get-tuple-element.23) | data formatting | bytes 39744
  58.3 0.7 %copy.30 = bf16[2,6,12,384]{3,0,2,1:T(2,128)(2,1)} copy(bf16[2,6,12,384]{3,2,1,0:T(8,128)(2,1)S(1)} %get-tuple-element.19) | data formatting | bytes 221184
  59.0 0.6 copy.35
  59.6 0.6 copy.36
  (4 shorter events, 0.0 us)
Async XLA Ops:
  3.6 6.1 %copy-start = (bf16[384,1152]{1,0:T(8,128)(2,1)S(1)}, bf16[384,1152]{1,0:T(8,128)(2,1)}, u32[]{:S(2)}) copy-start(bf16[384,1152]{1,0:T(8,128)(2,1)} %wqkv_hbm.1) | copy-start | bytes 2654212
  3.6 6.1 %copy-start.1 = (bf16[384,512]{1,0:T(8,128)(2,1)S(1)}, bf16[384,512]{1,0:T(8,128)(2,1)}, u32[]{:S(2)}) copy-start(bf16[384,512]{1,0:T(8,128)(2,1)} %constant.32.clone.rest_10_) | copy-start | bytes 1179652
  3.6 6.1 %copy-start.2 = (bf16[384,384]{1,0:T(8,128)(2,1)S(1)}, bf16[384,384]{1,0:T(8,128)(2,1)}, u32[]{:S(2)}) copy-start(bf16[384,384]{1,0:T(8,128)(2,1)} %wproj_hbm.1) | copy-start | bytes 884740
  3.6 6.1 %copy-start.3 = (bf16[2,192,288]{2,1,0:T(8,128)(2,1)S(1)}, bf16[2,192,288]{2,1,0:T(8,128)(2,1)}, u32[]{:S(2)}) copy-start(bf16[2,192,288]{2,1,0:T(8,128)(2,1)} %constant.28.clone.rest_6_) | copy-start | bytes 663556
  3.6 6.1 %copy-start.4 = (bf16[2,288,192]{2,1,0:T(8,128)(2,1)S(1)}, bf16[2,288,192]{2,1,0:T(8,128)(2,1)}, u32[]{:S(2)}) copy-start(bf16[2,288,192]{2,1,0:T(8,128)(2,1)} %constant.27.clone.rest_5_) | copy-start | bytes 663556
  3.6 6.0 %copy-start.5 = (bf16[384,320]{1,0:T(8,128)(2,1)S(1)}, bf16[384,320]{1,0:T(8,128)(2,1)}, u32[]{:S(2)}) copy-start(bf16[384,320]{1,0:T(8,128)(2,1)} %constant.23.clone.rest_1_) | copy-start | bytes 737284
  3.6 6.0 %copy-start.6 = (bf16[320,288]{1,0:T(8,128)(2,1)S(1)}, bf16[320,288]{1,0:T(8,128)(2,1)}, u32[]{:S(2)}) copy-start(bf16[320,288]{1,0:T(8,128)(2,1)} %constant.25.clone.rest_3_) | copy-start | bytes 552964
  3.7 6.0 %copy-start.7 = (bf16[320,384]{1,0:T(8,128)(2,1)S(1)}, bf16[320,384]{1,0:T(8,128)(2,1)}, u32[]{:S(2)}) copy-start(bf16[320,384]{1,0:T(8,128)(2,1)} %constant.22.clone.rest_0_) | copy-start | bytes 737284
  3.7 6.0 %copy-start.8 = (bf16[288,320]{1,0:T(8,128)(2,1)S(1)}, bf16[288,320]{1,0:T(8,128)(2,1)}, u32[]{:S(2)}) copy-start(bf16[288,320]{1,0:T(8,128)(2,1)} %constant.24.clone.rest_2_) | copy-start | bytes 552964
  3.7 6.0 %copy-start.9 = (bf16[128,144]{1,0:T(8,128)(2,1)S(1)}, bf16[128,144]{1,0:T(8,128)(2,1)}, u32[]{:S(2)}) copy-start(bf16[128,144]{1,0:T(8,128)(2,1)} %constant.31.clone.rest_9_) | copy-start | bytes 110596
  3.7 6.0 %copy-start.10 = (bf16[144,128]{1,0:T(8,128)(2,1)S(1)}, bf16[144,128]{1,0:T(8,128)(2,1)}, u32[]{:S(2)}) copy-start(bf16[144,128]{1,0:T(8,128)(2,1)} %constant.30.clone.rest_8_) | copy-start | bytes 110596
  3.7 6.0 %copy-start.11 = (bf16[144,16]{1,0:T(8,128)(2,1)S(1)}, bf16[144,16]{1,0:T(8,128)(2,1)}, u32[]{:S(2)}) copy-start(bf16[144,16]{1,0:T(8,128)(2,1)} %constant.29.clone.rest_7_) | copy-start | bytes 13828

commit v2 on v1

v2 whole, which is shorter than its diff:
```python
import functools

import jax
import jax.numpy as jnp
import numpy as np
from jax import lax
from jax.experimental import pallas as pl
from jax.experimental.pallas import tpu as pltpu
from jax.sharding import PartitionSpec as P

F32 = jnp.float32
BF16 = jnp.bfloat16
MESH = pl.DeviceIdType.MESH
SCALE = 32 ** (-0.5)


def patterns():
    order = np.zeros((144, 144), np.float32)
    toeplitz = np.zeros((6, 1024, 144), np.float32)
    dup = np.zeros((2, 288, 192), np.float32)
    key_rows = np.zeros((144, 16), np.float32)
    key_cols = np.zeros((144, 128), np.float32)
    halves = np.zeros((384, 384), np.float32)
    for l in range(2):
        for r in range(6):
            for c in range(12):
                p = 12 * c + 6 * l + r
                order[p, 24 * r + 2 * c + l] = 1
                key_rows[p, 2 * ((r + 3) % 6) + 1 - l] = 1
                key_cols[p, (c + 6) % 12] = 1
                for m in range(6):
                    for par in range(2):
                        spot = (2 * m + par + 6) % 12 - (c + 6) % 12 + 11
                        iq = (r + 3) % 6
                        lane = ((1 - l) * 2 + iq // 3) * 128 + (iq % 3) * 23 + spot
                        toeplitz[m, 512 * par + lane, p] = 1
    for h in range(12):
        for par in range(2):
            for l in range(2):
                for r in range(6):
                    zi = (1 - l) * 6 + (r + 3) % 6
                    dup[par, 24 * h + 12 * par + 6 * l + r, 16 * zi + h] = 1
    for f in range(384):
        i = f // 24
        halves[192 * (i % 2) + 24 * (i // 2) + f % 24, f] = 1
    both = [
        order,
        order.T,
        toeplitz,
        dup,
        dup.transpose(0, 2, 1),
        key_rows,
        key_cols,
        key_cols.T,
        halves,
    ]
    return [jnp.asarray(x, BF16) for x in both]


def dot(a, b, ca=1, cb=0):
    return lax.dot_general(a, b, (((ca,), (cb,)), ((), ())), preferred_element_type=F32)


def roll_left(value, by):
    width = value.shape[1]
    by = by % width
    return value if by == 0 else pltpu.roll(value, width - by, 1)


def kernel(
    in_hbm,
    cot_hbm,
    gain_hbm,
    wqkv_hbm,
    wproj_hbm,
    table_hbm,
    region_hbm,
    type_ref,
    *rest,
):
    const_hbm = rest[:9]
    out_ref, gin_ref, ggain_ref, gqkv_ref, gproj_ref, gbias_ref = rest[9:15]
    gain_ref, wqkv, wproj, table, region_ref = rest[15:20]
    const = rest[20:29]
    (
        win, win_cot, res, res_cot, tok, keys, trow, amat, bias, probs, gsb, gj, att,
        hs_own, hs_out, hs_in, as_own, as_out, as_in, gj_in, cw, cw_in,
        ysend, yrecv, xsend, xrecv, lsend, lrecv, bsend, brecv, asend, arecv,
        load_sem, own_sem, halo_s, halo_r, back_s, back_r, sib_s, sib_r, y_s, y_r, x_s, x_r,
        l_s, l_r, b_s, b_r, a_s, a_r,
    ) = rest[29:]
    order, order_t, toep, dup, dup_t, key_rows, key_cols, key_cols_t, halves = const

    i = lax.axis_index("lat")
    j = lax.axis_index("lon")
    y, x, core = i // 4, (i // 2) % 2, i % 2
    sibling = (i + 1 - 2 * core, j)
    up, down = (i + 15) % 16, (i + 1) % 16
    left, right = (j + 15) % 16, (j + 1) % 16

    def remote(src, dst, ssem, rsem, dev):
        return pltpu.make_async_remote_copy(
            src_ref=src, dst_ref=dst, send_sem=ssem, recv_sem=rsem,
            device_id=dev, device_id_type=MESH,
        )

    barrier = pltpu.get_barrier_semaphore()

    def greet(d, carry):
        pl.semaphore_signal(barrier, inc=1, device_id=((i + d) % 16, j), device_id_type=MESH)
        pl.semaphore_signal(barrier, inc=1, device_id=(i, (j + d) % 16), device_id_type=MESH)
        return carry

    pl.semaphore_signal(barrier, inc=1, device_id=(up, left), device_id_type=MESH)
    pl.semaphore_signal(barrier, inc=1, device_id=(down, right), device_id_type=MESH)
    lax.fori_loop(1, 16, greet, 0)

    own = [
        pltpu.make_async_copy(s.at[3:6, 6:12], d.at[3:6, 6:12], own_sem.at[n])
        for n, (s, d) in enumerate(((in_hbm, win), (cot_hbm, win_cot)))
    ]
    loads = [
        pltpu.make_async_copy(s, d, load_sem.at[n])
        for n, (s, d) in enumerate(
            zip(
                (table_hbm, region_hbm, gain_hbm, wqkv_hbm, wproj_hbm, *const_hbm),
                (table, region_ref, gain_ref, wqkv, wproj, *const),
            )
        )
    ]
    for c in (*own, *loads):
        c.start()

    corners = (
        ((slice(0, 3), slice(0, 6)), (up, left), (down, right)),
        ((slice(0, 3), slice(6, 12)), (up, j), (down, j)),
        ((slice(3, 6), slice(0, 6)), (i, left), (i, right)),
    )
    halo = [
        remote(s.at[spot], d.at[spot], halo_s.at[3 * n + k], halo_r.at[3 * n + k], dev)
        for n, (s, d) in enumerate(((in_hbm, win), (cot_hbm, win_cot)))
        for k, (spot, dev, _) in enumerate(corners)
    ]
    pl.semaphore_wait(barrier, 32)
    for c in halo:
        c.start()

    for c in loads:
        c.wait()
    for n in range(6):
        lat_side = (6 * i + n + 3 >= 96).astype(jnp.int32) * 2
        level = lax.broadcasted_iota(jnp.int32, (2, 12), 0)
        keys[2 * n : 2 * n + 2, 0:12] = (region_ref[n] * 4 + lat_side + level).astype(F32)
    in_grid = (lax.broadcasted_iota(jnp.int32, (16, 128), 0) < 12) & (
        lax.broadcasted_iota(jnp.int32, (16, 128), 1) < 12
    )
    key_grid = jnp.where(in_grid, keys[...], 0.0).astype(BF16)
    key_p = jnp.sum(
        dot(key_rows[...], key_grid) * key_cols[...].astype(F32), 1, keepdims=True
    )
    key_q = jnp.sum(
        dot(key_grid, key_rows[...], 0, 1) * key_cols_t[...].astype(F32), 0, keepdims=True
    )
    allowed = key_p == key_q

    kind = type_ref[0, 0]
    trow[...] = jnp.zeros((16, 3456), F32)
    is_kind = lax.broadcasted_iota(jnp.int32, (32, 3312), 0) == kind
    for h in range(12):
        trow[h : h + 1, 0:3312] = jnp.sum(
            jnp.where(is_kind, table[h].astype(F32), 0.0), 0, keepdims=True
        )
    for zp in range(2):
        for ip in range(6):
            for b in range(4):
                off = ((2 * zp + b // 2) * 36 + 6 * ip + 3 * (b % 2)) * 23
                a = off // 128 * 128
                piece = roll_left(trow[:, a : a + 256], off - a)[:, :128]
                row = (6 * zp + ip) * 16
                amat[row : row + 16, 128 * b : 128 * b + 128] = piece.astype(BF16)
    spread0 = dot(dup[0], amat[...]).astype(BF16)
    spread1 = dot(dup[1], amat[...]).astype(BF16)
    for m in range(6):
        part = dot(spread0, toep[m, 0:512]) + dot(spread1, toep[m, 512:1024])
        ok = allowed[24 * m : 24 * m + 24]
        for h in range(12):
            bias[h, 24 * m : 24 * m + 24, :] = jnp.where(ok, part[24 * h : 24 * h + 24], -1e30)

    def gather(source):
        for r in range(6):
            for c in range(12):
                k = 24 * r + 2 * c
                tok[k : k + 2, :] = source[r, c]
        return dot(order[...], tok[...])

    own[0].wait()
    for c in halo[0:3]:
        c.wait_recv()
    wide = gather(win)
    to_sib = [
        remote(src, dst, sib_s.at[n], sib_r.at[n], sibling)
        for n, (src, dst) in enumerate(
            [(cw, cw_in), (hs_out, hs_in), (as_out, as_in)]
            + [(gj.at[g], gj_in.at[g]) for g in range(3)]
        )
    ]

    def split_halves(value, own_half, out_half):
        spread = dot(halves[...], value, 1, 1).astype(BF16)
        first, second = spread[0:192], spread[192:384]
        own_half[...] = jnp.where(core == 0, first, second)
        out_half[...] = jnp.where(core == 0, second, first)

    def weight_part(n, left_own, left_in, right_own, right_in):
        part = dot(left_own[...], right_own) + dot(left_in[...], right_in)
        for k in range(4):
            ysend[n, k] = part[48 * k : 48 * k + 48].astype(BF16)

        def to_y(d):
            k = (y + d) % 4
            spot = 4 * n + d
            return remote(
                ysend.at[n, k], yrecv.at[n, d], y_s.at[spot], y_r.at[spot],
                (4 * k + 2 * x + core, j),
            )

        parts = [to_y(d) for d in range(1, 4)]
        for c in parts:
            c.start()
        return parts

    def put_back(value, target, n):
        back_rows = dot(order_t[...], value).astype(BF16)
        for r in range(6):
            for c in range(12):
                k = 24 * r + 2 * c
                target[r, c] = back_rows[k : k + 2]
        final = (out_ref, gin_ref)[n]
        sends = [
            remote(
                target.at[spot], final.at[spot],
                back_s.at[3 * n + k], back_r.at[3 * n + k], dev,
            )
            for k, (spot, _, dev) in enumerate(corners)
        ]
        kept = pltpu.make_async_copy(
            target.at[3:6, 6:12], final.at[3:6, 6:12], own_sem.at[2 + n]
        )
        for c in (*sends, kept):
            c.start()
        return sends, kept

    gain = gain_ref[...].reshape(1, 384)
    center = jnp.mean(wide, 1, keepdims=True)
    shifted = wide - center
    inv_std = lax.rsqrt(jnp.mean(jnp.square(shifted), 1, keepdims=True) + 1e-05)
    normed = shifted * inv_std
    hidden = (normed * gain).astype(BF16)
    joined = dot(hidden, wqkv[...]).astype(BF16)
    split_halves(hidden, hs_own, hs_out)
    to_sib[1].start()
    own[1].wait()
    for c in halo[3:6]:
        c.wait_recv()
    cw[...] = gather(win_cot).astype(BF16)
    to_sib[0].start()
    cot_rows = cw[...]
    grad_att = dot(cot_rows, wproj[...], 1, 1).astype(BF16)

    lane_head = lax.broadcasted_iota(jnp.int32, (1, 128), 1) // 32
    head_masks = [(lane_head == h).astype(F32).astype(BF16) for h in range(4)]
    wide_masks = [(lane_head == h).astype(F32) for h in range(4)]

    def pick(stacked):
        total = stacked[0:144] * wide_masks[0]
        for h in range(1, 4):
            total = total + stacked[144 * h : 144 * h + 144] * wide_masks[h]
        return total

    for g in range(3):
        lanes = slice(128 * g, 128 * g + 128)
        queries4 = jnp.concatenate([joined[:, lanes] * k for k in head_masks], 0)
        key_part = joined[:, 384 + 128 * g : 384 + 128 * g + 128]
        value_part = joined[:, 768 + 128 * g : 768 + 128 * g + 128]
        scores = dot(queries4, key_part, 1, 1) * SCALE
        scores = scores + bias[4 * g : 4 * g + 4].reshape(576, 144)
        top = jnp.max(scores, 1, keepdims=True)
        weights = jnp.exp(scores - top)
        weights = weights * (1.0 / jnp.sum(weights, 1, keepdims=True))
        probs[g] = weights
        att[:, lanes] = pick(dot(weights.astype(BF16), value_part)).astype(BF16)
    attended = att[...]
    split_halves(attended, as_own, as_out)
    to_sib[2].start()
    result = (wide + dot(attended, wproj[...])).astype(BF16)
    back_out, keep_out = put_back(result, res, 0)

    y_copies = []
    for g in range(3):
        lanes = slice(128 * g, 128 * g + 128)
        queries4 = jnp.concatenate([joined[:, lanes] * k for k in head_masks], 0)
        key_part = joined[:, 384 + 128 * g : 384 + 128 * g + 128]
        value_part = joined[:, 768 + 128 * g : 768 + 128 * g + 128]
        grad4 = jnp.concatenate([grad_att[:, lanes] * k for k in head_masks], 0)
        weights = probs[g]
        grad_probs = dot(grad4, value_part, 1, 1)
        grad_values = dot(weights.astype(BF16), grad4, 0, 0)
        grad_scores = weights * (grad_probs - jnp.sum(weights * grad_probs, 1, keepdims=True))
        for h in range(4):
            for m in range(6):
                row = 24 * (4 * g + h)
                gsb[m, row : row + 24, :] = grad_scores[144 * h + 24 * m : 144 * h + 24 * m + 24]
        grad_scaled = (grad_scores * SCALE).astype(BF16)
        grad_query = pick(dot(grad_scaled, key_part))
        grad_keys = dot(grad_scaled, queries4, 0, 0)
        gj[g, :, 0:128] = grad_query.astype(BF16)
        gj[g, :, 128:256] = grad_keys.astype(BF16)
        gj[g, :, 256:384] = grad_values.astype(BF16)
        to_sib[3 + g].start()
        if g == 0:
            to_sib[0].wait_recv()
            to_sib[2].wait_recv()
            y_copies.append(weight_part(0, as_own, as_in, cw[...], cw_in[...]))
            to_sib[1].wait_recv()
        else:
            to_sib[2 + g].wait_recv()
            y_copies.append(weight_part(g, hs_own, hs_in, gj[g - 1], gj_in[g - 1]))

    grad_joined = jnp.concatenate(
        [gj[g, :, 128 * n : 128 * n + 128] for n in range(3) for g in range(3)], 1
    )
    grad_hidden = dot(grad_joined, wqkv[...], 1, 1)
    to_sib[5].wait_recv()
    y_copies.append(weight_part(3, hs_own, hs_in, gj[2], gj_in[2]))

    grad_gain = jnp.sum(grad_hidden * normed, 0, keepdims=True)
    grad_normed = grad_hidden * gain
    grad_wide = inv_std * (
        grad_normed
        - jnp.mean(grad_normed, 1, keepdims=True)
        - normed * jnp.mean(grad_normed * normed, 1, keepdims=True)
    )
    grad_in = (cot_rows.astype(F32) + grad_wide).astype(BF16)
    back_grad, keep_grad = put_back(grad_in, res_cot, 1)

    folded = dot(gsb[0].astype(BF16), toep[0], 1, 1)
    for m in range(1, 6):
        folded = folded + dot(gsb[m].astype(BF16), toep[m], 1, 1)
    folded = folded.astype(BF16)
    shares = dot(dup_t[0], folded[:, 0:512]) + dot(dup_t[1], folded[:, 512:1024])
    share_row = lax.broadcasted_iota(jnp.int32, (16, 256), 0)
    share_lane = lax.broadcasted_iota(jnp.int32, (16, 256), 1)
    empty = jnp.zeros((16, 128), F32)

    def riders(gain_row, kind_row):
        high = gain_row.astype(BF16).astype(F32)
        low = gain_row - high
        rows = [
            high[:, 0:256],
            jnp.concatenate([high[:, 256:384], jnp.zeros((1, 128), F32)], 1),
            low[:, 0:256],
            jnp.concatenate([low[:, 256:384], jnp.zeros((1, 128), F32)], 1),
        ]
        block = jnp.where((share_row == 15) & (share_lane >= 128), kind_row, 0.0)
        for n, row in enumerate(rows):
            block = block + jnp.where(share_row == 12 + n, row, 0.0)
        return block

    def gain_of(block):
        return jnp.concatenate(
            [block[12:13] + block[14:15], block[13:14, 0:128] + block[15:16, 0:128]], 1
        )

    extra = riders(grad_gain, kind.astype(F32))
    for dest in range(16):
        zp, zq, k = dest // 8, (dest // 4) % 2, dest % 4
        block = extra
        for b in range(3):
            ip, iqh = (3 * k + b) // 2, (3 * k + b) % 2
            row, lane = (6 * zp + ip) * 16, (2 * zq + iqh) * 128
            piece = jnp.concatenate([shares[row : row + 16, lane : lane + 128], empty], 1)
            block = block + (pltpu.roll(piece, 69 * b, 1) if b else piece)
        bsend[dest] = block.astype(BF16)

    def bias_lon(d):
        to = (j + d) % 16
        return remote(bsend.at[to], brecv.at[d], b_s.at[d], b_r.at[d], (i, to))

    def start_all(make):
        def body(d, carry):
            make(d).start()
            return carry

        lax.fori_loop(1, 16, body, 0)

    def wait_all(make):
        def body(d, carry):
            make(d).wait_recv()
            return carry

        lax.fori_loop(1, 16, body, 0)

    def sent_all(make):
        def body(d, carry):
            make(d).wait_send()
            return carry

        lax.fori_loop(1, 16, body, 0)

    start_all(bias_lon)

    mine, x_copies = [], []
    for half in range(2):
        others = []
        for n in (2 * half, 2 * half + 1):
            for c in y_copies[n]:
                c.wait_recv()
            chunk = ysend[n, y].astype(F32)
            for d in range(1, 4):
                chunk = chunk + yrecv[n, d].astype(F32)
            mine.append(jnp.where(x == 0, chunk[0:24], chunk[24:48]))
            others.append(jnp.where(x == 0, chunk[24:48], chunk[0:24]))
        xsend[half] = jnp.concatenate(others, 0).astype(BF16)
        to_x = remote(
            xsend.at[half], xrecv.at[half], x_s.at[half], x_r.at[half],
            (4 * y + 2 * (1 - x) + core, j),
        )
        to_x.start()
        x_copies.append(to_x)

    wait_all(bias_lon)
    total = bsend[j].astype(F32)
    for d in range(1, 16):
        total = total + brecv[d].astype(F32)
    kinds = total[15:16, 128:129] * (1.0 / 16.0)
    block = jnp.where(share_row < 12, total, 0.0) + riders(gain_of(total), kinds)
    asend[...] = block.astype(BF16)

    def bias_lat(d):
        return remote(asend, arecv.at[d], a_s.at[d], a_r.at[d], ((i + d) % 16, j))

    start_all(bias_lat)

    for half, c in enumerate(x_copies):
        c.wait_recv()
        got = xrecv[half].astype(F32)
        mine[2 * half] = mine[2 * half] + got[0:24]
        mine[2 * half + 1] = mine[2 * half + 1] + got[24:48]
    own_qkv = jnp.concatenate(
        [mine[1 + g][:, 128 * n : 128 * n + 128] for n in range(3) for g in range(3)], 1
    )
    own_proj = mine[0]
    lane128 = lax.broadcasted_iota(jnp.int32, (24, 128), 1)
    for dest in range(16):
        off = 72 * dest
        a = min(off // 128 * 128, 896)
        piece = roll_left(own_qkv[:, a : a + 256], off - a)[:, :128]
        off = 24 * dest
        a = min(off // 128 * 128, 128)
        tail = roll_left(own_proj[:, a : a + 256], off - a - 72)[:, :128]
        block = jnp.where(lane128 < 72, piece, tail)
        block = jnp.concatenate([block, jnp.zeros((8, 128), F32)], 0)
        lsend[dest] = block.astype(BF16)

    def to_lon(d):
        to = (j + d) % 16
        return remote(lsend.at[to], lrecv.at[d], l_s.at[d], l_r.at[d], (i, to))

    start_all(to_lon)
    for c in (*halo, *to_sib, *back_out, *back_grad, *x_copies):
        c.wait_send()
    for parts in y_copies:
        for c in parts:
            c.wait_send()
    keep_out.wait()
    keep_grad.wait()
    sent_all(bias_lon)

    wait_all(bias_lat)
    gain_total = jnp.zeros((1, 384), F32)
    sums = [jnp.zeros((16, 256), F32), jnp.zeros((16, 256), F32)]
    for d in range(16):
        block = asend[...] if d == 0 else arecv[d]
        block = block.astype(F32)
        gain_total = gain_total + gain_of(block)
        for t in range(2):
            hit = block[15:16, 128:129] == (2 * i + t).astype(F32)
            sums[t] = sums[t] + jnp.where(hit, block, 0.0)
    ggain_ref[...] = gain_total.reshape(384)
    for h in range(12):
        row = jnp.concatenate([sums[0][h : h + 1, 0:207], sums[1][h : h + 1, 0:207]], 0)
        gbias_ref[h] = row
    sent_all(bias_lat)
    for c in (*back_out, *back_grad):
        c.wait_recv()

    wait_all(to_lon)
    total = lsend[j].astype(F32)
    for d in range(1, 16):
        total = total + lrecv[d].astype(F32)
    gqkv_ref[...] = total[0:24, 0:72]
    gproj_ref[...] = roll_left(total[0:24], 72)[:, 0:24]
    sent_all(to_lon)


def finish(*refs):
    for source, target in zip(refs[:6], refs[6:]):
        target[...] = source[...]


def local(inputs, cotangent, norm_gain, qkv_weight, proj_weight, bias_table, window_type, region):
    consts = patterns()
    vmem = pl.BlockSpec(memory_space=pltpu.VMEM)
    hbm = pl.BlockSpec(memory_space=pltpu.HBM)
    dma = pltpu.SemaphoreType.DMA
    tokens = (6, 12, 2, 384)
    shapes = [
        jax.ShapeDtypeStruct(tokens, BF16),
        jax.ShapeDtypeStruct(tokens, BF16),
        jax.ShapeDtypeStruct((384,), F32),
        jax.ShapeDtypeStruct((24, 72), F32),
        jax.ShapeDtypeStruct((24, 24), F32),
        jax.ShapeDtypeStruct((12, 2, 207), F32),
    ]
    outs = pl.pallas_call(
        kernel,
        out_shape=shapes,
        in_specs=[hbm] * 7 + [pl.BlockSpec(memory_space=pltpu.SMEM)] + [hbm] * len(consts),
        out_specs=[vmem] * 6,
        scratch_shapes=[
            pltpu.VMEM((384,), F32),
            pltpu.VMEM(qkv_weight.shape, BF16),
            pltpu.VMEM(proj_weight.shape, BF16),
            pltpu.VMEM((12, 32, 3312), BF16),
            pltpu.VMEM((6, 2, 12), jnp.int32),
        ]
        + [pltpu.VMEM(c.shape, BF16) for c in consts]
        + [
            pltpu.VMEM(tokens, BF16),
            pltpu.VMEM(tokens, BF16),
            pltpu.VMEM(tokens, BF16),
            pltpu.VMEM(tokens, BF16),
            pltpu.VMEM((144, 384), BF16),
            pltpu.VMEM((16, 128), F32),
            pltpu.VMEM((16, 3456), F32),
            pltpu.VMEM((192, 512), BF16),
            pltpu.VMEM((12, 144, 144), F32),
            pltpu.VMEM((3, 576, 144), F32),
            pltpu.VMEM((6, 288, 144), F32),
            pltpu.VMEM((3, 144, 384), BF16),
            pltpu.VMEM((144, 384), BF16),
            pltpu.VMEM((192, 144), BF16),
            pltpu.VMEM((192, 144), BF16),
            pltpu.VMEM((192, 144), BF16),
            pltpu.VMEM((192, 144), BF16),
            pltpu.VMEM((192, 144), BF16),
            pltpu.VMEM((192, 144), BF16),
            pltpu.VMEM((3, 144, 384), BF16),
            pltpu.VMEM((144, 384), BF16),
            pltpu.VMEM((144, 384), BF16),
            pltpu.VMEM((4, 4, 48, 384), BF16),
            pltpu.VMEM((4, 4, 48, 384), BF16),
            pltpu.VMEM((2, 48, 384), BF16),
            pltpu.VMEM((2, 48, 384), BF16),
            pltpu.VMEM((16, 32, 128), BF16),
            pltpu.VMEM((16, 32, 128), BF16),
            pltpu.VMEM((16, 16, 256), BF16),
            pltpu.VMEM((16, 16, 256), BF16),
            pltpu.VMEM((16, 256), BF16),
            pltpu.VMEM((16, 16, 256), BF16),
            dma((len(consts) + 5,)), dma((4,)),
            dma((6,)), dma((6,)), dma((6,)), dma((6,)), dma((6,)), dma((6,)),
            dma((16,)), dma((16,)), dma((2,)), dma((2,)),
            dma((16,)), dma((16,)), dma((16,)), dma((16,)), dma((16,)), dma((16,)),
        ],
        compiler_params=pltpu.CompilerParams(
            collective_id=0, has_side_effects=True, vmem_limit_bytes=62 * 2**20
        ),
    )(
        inputs.transpose(1, 2, 0, 3),
        cotangent.transpose(1, 2, 0, 3),
        norm_gain,
        qkv_weight,
        proj_weight,
        bias_table.transpose(1, 0, 2),
        region.transpose(1, 0, 2),
        window_type,
        *consts,
    )
    outs = pl.pallas_call(
        finish,
        out_shape=shapes,
        in_specs=[vmem] * 6,
        out_specs=[vmem] * 6,
    )(*outs)
    block_out, grad_inputs, grad_gain, grad_qkv, grad_proj, grad_bias = outs
    return (
        block_out.transpose(2, 0, 1, 3),
        grad_inputs.transpose(2, 0, 1, 3),
        grad_gain,
        grad_qkv,
        grad_proj,
        grad_bias.transpose(1, 0, 2),
    )


def solution(mesh):
    return jax.shard_map(
        local,
        mesh=mesh,
        in_specs=(
            P(None, "lat", "lon", None),
            P(None, "lat", "lon", None),
            P(),
            P(),
            P(),
            P(),
            P("lat", None),
            P(None, "lat", "lon"),
        ),
        out_specs=(
            P(None, "lat", "lon", None),
            P(None, "lat", "lon", None),
            P(),
            P("lat", "lon"),
            P("lat", "lon"),
            P("lat", None, "lon"),
        ),
        check_vma=False,
    )
```

time: 60.4 us -> 43.8 us (0.73)
  the two profiles are of different devices: /device:TPU:1 before, /device:TPU:2 now
where the time goes in v2:
time: 43.8 us; the launch traced here: 43.7 us
  Pallas kernels  42.4 us (97%)
  between operations  1.29 us (3%)
    pallas_call x1, Pallas kernels, local(): pl.pallas_call(kernel, out_shape=shapes, in_specs=[hbm] * 7 + [pl.BlockSp...  40.7 us
    pallas_call x1, Pallas kernels, local(): pl.pallas_call(finish, out_shape=shapes, in_specs=[vmem] * 6, out_specs=[...  1.73 us

profile of v2, /device:TPU:2, one launch (start us, length us, event | category | flops | bytes accessed | tf_op | source)
XLA Modules:
  0.0 43.7 jit_solution(5861398872028896247)
XLA Ops:
  1.3 40.7 %shard_map.208 = (bf16[6,12,2,384]{3,2,1,0:T(2,128)(2,1)}, bf16[6,12,2,384]{3,2,1,0:T(2,128)(2,1)}, f32[384]{0:T(512)}, f32[24,72]{1,0:T(8,128)}, f32[24,24]{1,0:T(8,128)}, /*index=5*/f32[12,2,207]{2,1,0:T(2,128)}) custom-call(bf16[6,12,2,384]{3,2,1,0:T(2,128)(2,1)} %bitcast.8, bf16[6,12,2,384]{3,2,1,0:T(2,128)(2,1)} %bitcast.9, f32[384]{0:T(512)} %gain_hbm.1, ...), custom_call_target="tpu_custom_call" | custom-call | tf_op jit(solution)/shard_map/pallas_call | solution.py:525
  42.0 1.7 %shard_map.209 = (bf16[6,12,2,384]{3,2,1,0:T(2,128)(2,1)}, bf16[6,12,2,384]{3,2,1,0:T(2,128)(2,1)}, f32[384]{0:T(512)}, f32[24,72]{1,0:T(8,128)}, f32[24,24]{1,0:T(8,128)}, /*index=5*/f32[12,2,207]{2,1,0:T(2,128)}) custom-call(bf16[6,12,2,384]{3,2,1,0:T(2,128)(2,1)} %get-tuple-element.18.refs_0_, bf16[6,12,2,384]{3,2,1,0:T(2,128)(2,1)} %get-tuple-element.19.refs_1_, ...), custom_call_target="tpu_custom_call" | custom-call | tf_op jit(solution)/shard_map/pallas_call | solution.py:590

commit v3 on v2

--- a/solution.py
+++ b/solution.py
@@ -16,7 +16,7 @@
 
 def patterns():
     order = np.zeros((144, 144), np.float32)
-    toeplitz = np.zeros((6, 1024, 144), np.float32)
+    toeplitz = np.zeros((6, 144, 768), np.float32)
     dup = np.zeros((2, 288, 192), np.float32)
     key_rows = np.zeros((144, 16), np.float32)
     key_cols = np.zeros((144, 128), np.float32)
@@ -32,8 +32,8 @@
                     for par in range(2):
                         spot = (2 * m + par + 6) % 12 - (c + 6) % 12 + 11
                         iq = (r + 3) % 6
-                        lane = ((1 - l) * 2 + iq // 3) * 128 + (iq % 3) * 23 + spot
-                        toeplitz[m, 512 * par + lane, p] = 1
+                        lane = (1 - l) * 138 + iq * 23 + spot
+                        toeplitz[m, p, 384 * par + lane] = 1
     for h in range(12):
         for par in range(2):
             for l in range(2):
@@ -44,15 +44,15 @@
         i = f // 24
         halves[192 * (i % 2) + 24 * (i // 2) + f % 24, f] = 1
     both = [
-        order,
-        order.T,
-        toeplitz,
-        dup,
-        dup.transpose(0, 2, 1),
         key_rows,
         key_cols,
         key_cols.T,
+        dup,
+        toeplitz,
+        order,
         halves,
+        order.T,
+        dup.transpose(0, 2, 1),
     ]
     return [jnp.asarray(x, BF16) for x in both]
 
@@ -83,13 +83,13 @@
     gain_ref, wqkv, wproj, table, region_ref = rest[15:20]
     const = rest[20:29]
     (
-        win, win_cot, res, res_cot, tok, keys, trow, amat, bias, probs, gsb, gj, att,
-        hs_own, hs_out, hs_in, as_own, as_out, as_in, gj_in, cw, cw_in,
-        ysend, yrecv, xsend, xrecv, lsend, lrecv, bsend, brecv, asend, arecv,
-        load_sem, own_sem, halo_s, halo_r, back_s, back_r, sib_s, sib_r, y_s, y_r, x_s, x_r,
+        win, win_cot, res, res_cot, out_own, gin_own, tok, keys, trow, amat, bias, probs, gsb, gqk, gv, att,
+        hs_own, hs_out, hs_in, as_own, as_out, as_in, gqk_in, gv_in, cw, cw_in,
+        ysend, yrecv, zsend, zrecv, xsend, xrecv, lsend, lrecv, bsend, brecv, asend, arecv,
+        load_sem, own_sem, halo_s, halo_r, back_s, back_r, sib_s, sib_r, y_s, y_r, z_s, z_r, x_s, x_r,
         l_s, l_r, b_s, b_r, a_s, a_r,
     ) = rest[29:]
-    order, order_t, toep, dup, dup_t, key_rows, key_cols, key_cols_t, halves = const
+    key_rows, key_cols, key_cols_t, dup, toep, order, halves, order_t, dup_t = const
 
     i = lax.axis_index("lat")
     j = lax.axis_index("lon")
@@ -105,14 +105,14 @@
         )
 
     barrier = pltpu.get_barrier_semaphore()
+    for dev in ((up, left), (down, right)):
+        pl.semaphore_signal(barrier, inc=1, device_id=dev, device_id_type=MESH)
 
     def greet(d, carry):
         pl.semaphore_signal(barrier, inc=1, device_id=((i + d) % 16, j), device_id_type=MESH)
         pl.semaphore_signal(barrier, inc=1, device_id=(i, (j + d) % 16), device_id_type=MESH)
         return carry
 
-    pl.semaphore_signal(barrier, inc=1, device_id=(up, left), device_id_type=MESH)
-    pl.semaphore_signal(barrier, inc=1, device_id=(down, right), device_id_type=MESH)
     lax.fori_loop(1, 16, greet, 0)
 
     own = [
@@ -123,8 +123,8 @@
         pltpu.make_async_copy(s, d, load_sem.at[n])
         for n, (s, d) in enumerate(
             zip(
-                (table_hbm, region_hbm, gain_hbm, wqkv_hbm, wproj_hbm, *const_hbm),
-                (table, region_ref, gain_ref, wqkv, wproj, *const),
+                (region_hbm, *const_hbm[:3], table_hbm, *const_hbm[3:6], gain_hbm, wqkv_hbm, const_hbm[6], wproj_hbm, *const_hbm[7:]),
+                (region_ref, *const[:3], table, *const[3:6], gain_ref, wqkv, const[6], wproj, *const[7:]),
             )
         )
     ]
@@ -145,7 +145,7 @@
     for c in halo:
         c.start()
 
-    for c in loads:
+    for c in loads[0:4]:
         c.wait()
     for n in range(6):
         lat_side = (6 * i + n + 3 >= 96).astype(jnp.int32) * 2
@@ -166,25 +166,31 @@
     kind = type_ref[0, 0]
     trow[...] = jnp.zeros((16, 3456), F32)
     is_kind = lax.broadcasted_iota(jnp.int32, (32, 3312), 0) == kind
+    loads[4].wait()
     for h in range(12):
         trow[h : h + 1, 0:3312] = jnp.sum(
             jnp.where(is_kind, table[h].astype(F32), 0.0), 0, keepdims=True
         )
+    wide_lane = lax.broadcasted_iota(jnp.int32, (16, 384), 1)
     for zp in range(2):
         for ip in range(6):
-            for b in range(4):
-                off = ((2 * zp + b // 2) * 36 + 6 * ip + 3 * (b % 2)) * 23
+            pieces = []
+            for zq in range(2):
+                off = ((2 * zp + zq) * 36 + 6 * ip) * 23
                 a = off // 128 * 128
-                piece = roll_left(trow[:, a : a + 256], off - a)[:, :128]
-                row = (6 * zp + ip) * 16
-                amat[row : row + 16, 128 * b : 128 * b + 128] = piece.astype(BF16)
-    spread0 = dot(dup[0], amat[...]).astype(BF16)
-    spread1 = dot(dup[1], amat[...]).astype(BF16)
+                pieces.append(roll_left(trow[:, a : a + 384], off - a - 138 * zq))
+            row = (6 * zp + ip) * 16
+            amat[row : row + 16, :] = jnp.where(wide_lane < 138, *pieces).astype(BF16)
+    loads[5].wait()
+    spread = jnp.concatenate([dot(dup[0], amat[...]), dot(dup[1], amat[...])], 1).astype(BF16)
+    loads[6].wait()
     for m in range(6):
-        part = dot(spread0, toep[m, 0:512]) + dot(spread1, toep[m, 512:1024])
+        part = dot(spread, toep[m], 1, 1)
         ok = allowed[24 * m : 24 * m + 24]
         for h in range(12):
             bias[h, 24 * m : 24 * m + 24, :] = jnp.where(ok, part[24 * h : 24 * h + 24], -1e30)
+    for c in loads[7:]:
+        c.wait()
 
     def gather(source):
         for r in range(6):
@@ -192,6 +198,7 @@
                 k = 24 * r + 2 * c
                 tok[k : k + 2, :] = source[r, c]
         return dot(order[...], tok[...])
+
 
     own[0].wait()
     for c in halo[0:3]:
@@ -200,8 +207,8 @@
     to_sib = [
         remote(src, dst, sib_s.at[n], sib_r.at[n], sibling)
         for n, (src, dst) in enumerate(
-            [(cw, cw_in), (hs_out, hs_in), (as_out, as_in)]
-            + [(gj.at[g], gj_in.at[g]) for g in range(3)]
+            [(cw, cw_in), (hs_out, hs_in), (as_out, as_in), (gv, gv_in)]
+            + [(gqk.at[g], gqk_in.at[g]) for g in range(3)]
         )
     ]
 
@@ -211,44 +218,75 @@
         own_half[...] = jnp.where(core == 0, first, second)
         out_half[...] = jnp.where(core == 0, second, first)
 
+    def whole(ref, ssem, rsem):
+        return [pltpu.make_async_copy(ref, ref, sem) for sem in (ssem, rsem)]
+
     def weight_part(n, left_own, left_in, right_own, right_in):
         part = dot(left_own[...], right_own) + dot(left_in[...], right_in)
-        for k in range(4):
-            ysend[n, k] = part[48 * k : 48 * k + 48].astype(BF16)
-
-        def to_y(d):
-            k = (y + d) % 4
-            spot = 4 * n + d
-            return remote(
-                ysend.at[n, k], yrecv.at[n, d], y_s.at[spot], y_r.at[spot],
-                (4 * k + 2 * x + core, j),
-            )
-
-        parts = [to_y(d) for d in range(1, 4)]
+        if n >= 2:
+            q = n - 2
+            for k in range(8):
+                rows = part[24 * k : 24 * k + 24]
+                zsend[q, k] = jnp.concatenate([rows[:, 0:128], rows[:, 128:256]], 0).astype(BF16)
+
+            def to_lat(d):
+                k = 2 * ((y + d // 2) % 4) + (x + d) % 2
+                return remote(
+                    zsend.at[q, k], zrecv.at[q, d], z_s.at[q], z_r.at[q], (2 * k + core, j)
+                )
+
+            parts = [to_lat(d) for d in range(1, 8)]
+            waits = whole(zrecv.at[q, pl.ds(1, 7)], z_s.at[q], z_r.at[q])
+        else:
+            for k in range(4):
+                ysend[n, k] = part[48 * k : 48 * k + 48].astype(BF16)
+
+            def to_y(d):
+                k = (y + d) % 4
+                return remote(
+                    ysend.at[n, k], yrecv.at[n, d], y_s.at[n], y_r.at[n],
+                    (4 * k + 2 * x + core, j),
+                )
+
+            parts = [to_y(d) for d in range(1, 4)]
+            waits = whole(yrecv.at[n, pl.ds(1, 3)], y_s.at[n], y_r.at[n])
         for c in parts:
             c.start()
-        return parts
+        return waits
+
+    def over_x():
+        keep, others = [], []
+        for n in range(2):
+            y_copies[n][1].wait()
+            chunk = ysend[n, y].astype(F32)
+            for d in range(1, 4):
+                chunk = chunk + yrecv[n, d].astype(F32)
+            keep.append(jnp.where(x == 0, chunk[0:24], chunk[24:48]))
+            others.append(jnp.where(x == 0, chunk[24:48], chunk[0:24]))
+        xsend[...] = jnp.concatenate(others, 0).astype(BF16)
+        to_x = remote(xsend, xrecv, x_s, x_r, (4 * y + 2 * (1 - x) + core, j))
+        to_x.start()
+        return keep, to_x
+
+    landed = (out_own, gin_own)
 
     def put_back(value, target, n):
         back_rows = dot(order_t[...], value).astype(BF16)
         for r in range(6):
             for c in range(12):
                 k = 24 * r + 2 * c
-                target[r, c] = back_rows[k : k + 2]
-        final = (out_ref, gin_ref)[n]
+                kept = r >= 3 and c >= 6
+                (landed[n] if kept else target)[r, c] = back_rows[k : k + 2]
         sends = [
             remote(
-                target.at[spot], final.at[spot],
+                target.at[spot], landed[n].at[spot],
                 back_s.at[3 * n + k], back_r.at[3 * n + k], dev,
             )
             for k, (spot, _, dev) in enumerate(corners)
         ]
-        kept = pltpu.make_async_copy(
-            target.at[3:6, 6:12], final.at[3:6, 6:12], own_sem.at[2 + n]
-        )
-        for c in (*sends, kept):
+        for c in sends:
             c.start()
-        return sends, kept
+        return sends
 
     gain = gain_ref[...].reshape(1, 384)
     center = jnp.mean(wide, 1, keepdims=True)
@@ -288,14 +326,24 @@
         weights = jnp.exp(scores - top)
         weights = weights * (1.0 / jnp.sum(weights, 1, keepdims=True))
         probs[g] = weights
-        att[:, lanes] = pick(dot(weights.astype(BF16), value_part)).astype(BF16)
+        probs_low = weights.astype(BF16)
+        att[:, lanes] = pick(dot(probs_low, value_part)).astype(BF16)
+        grad4 = jnp.concatenate([grad_att[:, lanes] * k for k in head_masks], 0)
+        gv[:, lanes] = dot(probs_low, grad4, 0, 0).astype(BF16)
+    to_sib[3].start()
     attended = att[...]
     split_halves(attended, as_own, as_out)
     to_sib[2].start()
+
     result = (wide + dot(attended, wproj[...])).astype(BF16)
-    back_out, keep_out = put_back(result, res, 0)
-
-    y_copies = []
+    back_out = put_back(result, res, 0)
+
+    to_sib[1].wait_recv()
+    to_sib[3].wait_recv()
+    y_copies = [weight_part(0, hs_own, hs_in, gv[...], gv_in[...])]
+    to_sib[0].wait_recv()
+    to_sib[2].wait_recv()
+    y_copies.append(weight_part(1, as_own, as_in, cw[...], cw_in[...]))
     for g in range(3):
         lanes = slice(128 * g, 128 * g + 128)
         queries4 = jnp.concatenate([joined[:, lanes] * k for k in head_masks], 0)
@@ -304,7 +352,6 @@
         grad4 = jnp.concatenate([grad_att[:, lanes] * k for k in head_masks], 0)
         weights = probs[g]
         grad_probs = dot(grad4, value_part, 1, 1)
-        grad_values = dot(weights.astype(BF16), grad4, 0, 0)
         grad_scores = weights * (grad_probs - jnp.sum(weights * grad_probs, 1, keepdims=True))
         for h in range(4):
             for m in range(6):
@@ -313,44 +360,26 @@
         grad_scaled = (grad_scores * SCALE).astype(BF16)
         grad_query = pick(dot(grad_scaled, key_part))
         grad_keys = dot(grad_scaled, queries4, 0, 0)
-        gj[g, :, 0:128] = grad_query.astype(BF16)
-        gj[g, :, 128:256] = grad_keys.astype(BF16)
-        gj[g, :, 256:384] = grad_values.astype(BF16)
-        to_sib[3 + g].start()
-        if g == 0:
-            to_sib[0].wait_recv()
-            to_sib[2].wait_recv()
-            y_copies.append(weight_part(0, as_own, as_in, cw[...], cw_in[...]))
-            to_sib[1].wait_recv()
-        else:
-            to_sib[2 + g].wait_recv()
-            y_copies.append(weight_part(g, hs_own, hs_in, gj[g - 1], gj_in[g - 1]))
+        gqk[g, :, 0:128] = grad_query.astype(BF16)
+        gqk[g, :, 128:256] = grad_keys.astype(BF16)
+        to_sib[4 + g].start()
+        if g > 0:
+            to_sib[3 + g].wait_recv()
+            y_copies.append(weight_part(1 + g, hs_own, hs_in, gqk[g - 1], gqk_in[g - 1]))
 
     grad_joined = jnp.concatenate(
-        [gj[g, :, 128 * n : 128 * n + 128] for n in range(3) for g in range(3)], 1
+        [gqk[g, :, 128 * n : 128 * n + 128] for n in range(2) for g in range(3)] + [gv[...]], 1
     )
     grad_hidden = dot(grad_joined, wqkv[...], 1, 1)
-    to_sib[5].wait_recv()
-    y_copies.append(weight_part(3, hs_own, hs_in, gj[2], gj_in[2]))
-
     grad_gain = jnp.sum(grad_hidden * normed, 0, keepdims=True)
-    grad_normed = grad_hidden * gain
-    grad_wide = inv_std * (
-        grad_normed
-        - jnp.mean(grad_normed, 1, keepdims=True)
-        - normed * jnp.mean(grad_normed * normed, 1, keepdims=True)
-    )
-    grad_in = (cot_rows.astype(F32) + grad_wide).astype(BF16)
-    back_grad, keep_grad = put_back(grad_in, res_cot, 1)
-
-    folded = dot(gsb[0].astype(BF16), toep[0], 1, 1)
+    folded = dot(gsb[0].astype(BF16), toep[0])
     for m in range(1, 6):
-        folded = folded + dot(gsb[m].astype(BF16), toep[m], 1, 1)
+        folded = folded + dot(gsb[m].astype(BF16), toep[m])
     folded = folded.astype(BF16)
-    shares = dot(dup_t[0], folded[:, 0:512]) + dot(dup_t[1], folded[:, 512:1024])
+
+    shares = dot(dup_t[0], folded[:, 0:384]) + dot(dup_t[1], folded[:, 384:768])
     share_row = lax.broadcasted_iota(jnp.int32, (16, 256), 0)
     share_lane = lax.broadcasted_iota(jnp.int32, (16, 256), 1)
-    empty = jnp.zeros((16, 128), F32)
 
     def riders(gain_row, kind_row):
         high = gain_row.astype(BF16).astype(F32)
@@ -374,17 +403,19 @@
     extra = riders(grad_gain, kind.astype(F32))
     for dest in range(16):
         zp, zq, k = dest // 8, (dest // 4) % 2, dest % 4
-        block = extra
-        for b in range(3):
-            ip, iqh = (3 * k + b) // 2, (3 * k + b) % 2
-            row, lane = (6 * zp + ip) * 16, (2 * zq + iqh) * 128
-            piece = jnp.concatenate([shares[row : row + 16, lane : lane + 128], empty], 1)
-            block = block + (pltpu.roll(piece, 69 * b, 1) if b else piece)
+        first = (6 * zp + 3 * k // 2) * 16
+        edge = 69 if k % 2 else 138
+        pieces = [
+            roll_left(shares[row : row + 16], 138 * zq + start)[:, 0:256]
+            for row, start in ((first, 138 - edge), (first + 16, -edge))
+        ]
+        block = jnp.where(share_lane < edge, *pieces)
+        block = jnp.where((share_row < 12) & (share_lane < 207), block, 0.0) + extra
         bsend[dest] = block.astype(BF16)
 
     def bias_lon(d):
         to = (j + d) % 16
-        return remote(bsend.at[to], brecv.at[d], b_s.at[d], b_r.at[d], (i, to))
+        return remote(bsend.at[to], brecv.at[d], b_s, b_r, (i, to))
 
     def start_all(make):
         def body(d, carry):
@@ -393,63 +424,39 @@
 
         lax.fori_loop(1, 16, body, 0)
 
-    def wait_all(make):
-        def body(d, carry):
-            make(d).wait_recv()
-            return carry
-
-        lax.fori_loop(1, 16, body, 0)
-
-    def sent_all(make):
-        def body(d, carry):
-            make(d).wait_send()
-            return carry
-
-        lax.fori_loop(1, 16, body, 0)
-
+    all_lon = whole(lrecv.at[pl.ds(1, 15)], l_s, l_r)
+    all_bias = whole(brecv.at[pl.ds(1, 15)], b_s, b_r)
+    all_lat = whole(arecv.at[pl.ds(1, 15)], a_s, a_r)
     start_all(bias_lon)
 
-    mine, x_copies = [], []
-    for half in range(2):
-        others = []
-        for n in (2 * half, 2 * half + 1):
-            for c in y_copies[n]:
-                c.wait_recv()
-            chunk = ysend[n, y].astype(F32)
-            for d in range(1, 4):
-                chunk = chunk + yrecv[n, d].astype(F32)
-            mine.append(jnp.where(x == 0, chunk[0:24], chunk[24:48]))
-            others.append(jnp.where(x == 0, chunk[24:48], chunk[0:24]))
-        xsend[half] = jnp.concatenate(others, 0).astype(BF16)
-        to_x = remote(
-            xsend.at[half], xrecv.at[half], x_s.at[half], x_r.at[half],
-            (4 * y + 2 * (1 - x) + core, j),
-        )
-        to_x.start()
-        x_copies.append(to_x)
-
-    wait_all(bias_lon)
-    total = bsend[j].astype(F32)
-    for d in range(1, 16):
-        total = total + brecv[d].astype(F32)
-    kinds = total[15:16, 128:129] * (1.0 / 16.0)
-    block = jnp.where(share_row < 12, total, 0.0) + riders(gain_of(total), kinds)
-    asend[...] = block.astype(BF16)
-
-    def bias_lat(d):
-        return remote(asend, arecv.at[d], a_s.at[d], a_r.at[d], ((i + d) % 16, j))
-
-    start_all(bias_lat)
-
-    for half, c in enumerate(x_copies):
-        c.wait_recv()
-        got = xrecv[half].astype(F32)
-        mine[2 * half] = mine[2 * half] + got[0:24]
-        mine[2 * half + 1] = mine[2 * half + 1] + got[24:48]
+    to_sib[6].wait_recv()
+    y_copies.append(weight_part(4, hs_own, hs_in, gqk[2], gqk_in[2]))
+
+    mine, to_x = over_x()
+    grad_normed = grad_hidden * gain
+    grad_wide = inv_std * (
+        grad_normed
+        - jnp.mean(grad_normed, 1, keepdims=True)
+        - normed * jnp.mean(grad_normed * normed, 1, keepdims=True)
+    )
+    grad_in = (cot_rows.astype(F32) + grad_wide).astype(BF16)
+    back_grad = put_back(grad_in, res_cot, 1)
+
+    own_qk = []
+    for q in range(3):
+        y_copies[2 + q][1].wait()
+        chunk = zsend[q, 2 * y + x].astype(F32)
+        for d in range(1, 8):
+            chunk = chunk + zrecv[q, d].astype(F32)
+        own_qk.append(chunk)
+    to_x.wait_recv()
+    got = xrecv[...].astype(F32)
+    own_value = mine[0] + got[0:24]
+    own_proj = mine[1] + got[24:48]
     own_qkv = jnp.concatenate(
-        [mine[1 + g][:, 128 * n : 128 * n + 128] for n in range(3) for g in range(3)], 1
-    )
-    own_proj = mine[0]
+        [part[0:24] for part in own_qk] + [part[24:48] for part in own_qk] + [own_value],
+        1,
+    )
     lane128 = lax.broadcasted_iota(jnp.int32, (24, 128), 1)
     for dest in range(16):
         off = 72 * dest
@@ -464,19 +471,30 @@
 
     def to_lon(d):
         to = (j + d) % 16
-        return remote(lsend.at[to], lrecv.at[d], l_s.at[d], l_r.at[d], (i, to))
+        return remote(lsend.at[to], lrecv.at[d], l_s, l_r, (i, to))
 
     start_all(to_lon)
-    for c in (*halo, *to_sib, *back_out, *back_grad, *x_copies):
+
+    all_bias[1].wait()
+    total = bsend[j].astype(F32)
+    for d in range(1, 16):
+        total = total + brecv[d].astype(F32)
+    kinds = total[15:16, 128:129] * (1.0 / 16.0)
+    block = jnp.where(share_row < 12, total, 0.0) + riders(gain_of(total), kinds)
+    asend[...] = block.astype(BF16)
+
+    def bias_lat(d):
+        return remote(asend, arecv.at[d], a_s, a_r, ((i + d) % 16, j))
+
+    start_all(bias_lat)
+
+    for c in (*halo, *to_sib, *back_out, *back_grad, to_x):
         c.wait_send()
-    for parts in y_copies:
-        for c in parts:
-            c.wait_send()
-    keep_out.wait()
-    keep_grad.wait()
-    sent_all(bias_lon)
-
-    wait_all(bias_lat)
+    for sent, _ in y_copies:
+        sent.wait()
+    all_bias[0].wait()
+
+    all_lat[1].wait()
     gain_total = jnp.zeros((1, 384), F32)
     sums = [jnp.zeros((16, 256), F32), jnp.zeros((16, 256), F32)]
     for d in range(16):
@@ -490,17 +508,23 @@
     for h in range(12):
         row = jnp.concatenate([sums[0][h : h + 1, 0:207], sums[1][h : h + 1, 0:207]], 0)
         gbias_ref[h] = row
-    sent_all(bias_lat)
-    for c in (*back_out, *back_grad):
-        c.wait_recv()
-
-    wait_all(to_lon)
+    all_lat[0].wait()
+    writes = []
+    for n, (copies, target) in enumerate(((back_out, out_ref), (back_grad, gin_ref))):
+        for c in copies:
+            c.wait_recv()
+        writes.append(pltpu.make_async_copy(landed[n], target, own_sem.at[2 + n]))
+        writes[n].start()
+
+    all_lon[1].wait()
     total = lsend[j].astype(F32)
     for d in range(1, 16):
         total = total + lrecv[d].astype(F32)
     gqkv_ref[...] = total[0:24, 0:72]
     gproj_ref[...] = roll_left(total[0:24], 72)[:, 0:24]
-    sent_all(to_lon)
+    all_lon[0].wait()
+    for c in writes:
+        c.wait()
 
 
 def finish(*refs):
@@ -526,7 +550,7 @@
         kernel,
         out_shape=shapes,
         in_specs=[hbm] * 7 + [pl.BlockSpec(memory_space=pltpu.SMEM)] + [hbm] * len(consts),
-        out_specs=[vmem] * 6,
+        out_specs=[hbm] * 2 + [vmem] * 4,
         scratch_shapes=[
             pltpu.VMEM((384,), F32),
             pltpu.VMEM(qkv_weight.shape, BF16),
@@ -540,14 +564,17 @@
             pltpu.VMEM(tokens, BF16),
             pltpu.VMEM(tokens, BF16),
             pltpu.VMEM(tokens, BF16),
+            pltpu.VMEM(tokens, BF16),
+            pltpu.VMEM(tokens, BF16),
             pltpu.VMEM((144, 384), BF16),
             pltpu.VMEM((16, 128), F32),
             pltpu.VMEM((16, 3456), F32),
-            pltpu.VMEM((192, 512), BF16),
+            pltpu.VMEM((192, 384), BF16),
             pltpu.VMEM((12, 144, 144), F32),
             pltpu.VMEM((3, 576, 144), F32),
             pltpu.VMEM((6, 288, 144), F32),
-            pltpu.VMEM((3, 144, 384), BF16),
+            pltpu.VMEM((3, 144, 256), BF16),
+            pltpu.VMEM((144, 384), BF16),
             pltpu.VMEM((144, 384), BF16),
             pltpu.VMEM((192, 144), BF16),
             pltpu.VMEM((192, 144), BF16),
@@ -555,13 +582,16 @@
             pltpu.VMEM((192, 144), BF16),
             pltpu.VMEM((192, 144), BF16),
             pltpu.VMEM((192, 144), BF16),
-            pltpu.VMEM((3, 144, 384), BF16),
+            pltpu.VMEM((3, 144, 256), BF16),
             pltpu.VMEM((144, 384), BF16),
             pltpu.VMEM((144, 384), BF16),
-            pltpu.VMEM((4, 4, 48, 384), BF16),
-            pltpu.VMEM((4, 4, 48, 384), BF16),
-            pltpu.VMEM((2, 48, 384), BF16),
-            pltpu.VMEM((2, 48, 384), BF16),
+            pltpu.VMEM((144, 384), BF16),
+            pltpu.VMEM((2, 4, 48, 384), BF16),
+            pltpu.VMEM((2, 4, 48, 384), BF16),
+            pltpu.VMEM((3, 8, 48, 128), BF16),
+            pltpu.VMEM((3, 8, 48, 128), BF16),
+            pltpu.VMEM((48, 384), BF16),
+            pltpu.VMEM((48, 384), BF16),
             pltpu.VMEM((16, 32, 128), BF16),
             pltpu.VMEM((16, 32, 128), BF16),
             pltpu.VMEM((16, 16, 256), BF16),
@@ -569,9 +599,9 @@
             pltpu.VMEM((16, 256), BF16),
             pltpu.VMEM((16, 16, 256), BF16),
             dma((len(consts) + 5,)), dma((4,)),
-            dma((6,)), dma((6,)), dma((6,)), dma((6,)), dma((6,)), dma((6,)),
-            dma((16,)), dma((16,)), dma((2,)), dma((2,)),
-            dma((16,)), dma((16,)), dma((16,)), dma((16,)), dma((16,)), dma((16,)),
+            dma((6,)), dma((6,)), dma((6,)), dma((6,)), dma((7,)), dma((7,)),
+            dma((2,)), dma((2,)), dma((3,)), dma((3,)), dma, dma,
+            dma, dma, dma, dma, dma, dma,
         ],
         compiler_params=pltpu.CompilerParams(
             collective_id=0, has_side_effects=True, vmem_limit_bytes=62 * 2**20

time: 43.8 us -> 42.8 us (0.977)
  the two profiles are of different devices: /device:TPU:2 before, /device:TPU:1 now
where the time goes in v3:
time: 42.8 us; the launch traced here: 42.7 us
  Pallas kernels  41.4 us (97%)
  between operations  1.29 us (3%)
    pallas_call x1, Pallas kernels, local(): pl.pallas_call(kernel, out_shape=shapes, in_specs=[hbm] * 7 + [pl.BlockSp...  39.7 us
    pallas_call x1, Pallas kernels, local(): pl.pallas_call(finish, out_shape=shapes, in_specs=[vmem] * 6, out_specs=[...  1.73 us

profile of v3, /device:TPU:1, one launch (start us, length us, event | category | flops | bytes accessed | tf_op | source)
XLA Modules:
  0.0 42.7 jit_solution(10582632282570240408)
XLA Ops:
  1.3 39.7 %shard_map.208 = (bf16[6,12,2,384]{3,2,1,0:T(2,128)(2,1)}, bf16[6,12,2,384]{3,2,1,0:T(2,128)(2,1)}, f32[384]{0:T(512)}, f32[24,72]{1,0:T(8,128)}, f32[24,24]{1,0:T(8,128)}, /*index=5*/f32[12,2,207]{2,1,0:T(2,128)}) custom-call(bf16[6,12,2,384]{3,2,1,0:T(2,128)(2,1)} %bitcast.8, bf16[6,12,2,384]{3,2,1,0:T(2,128)(2,1)} %bitcast.9, f32[384]{0:T(512)} %gain_hbm.1, ...), custom_call_target="tpu_custom_call" | custom-call | tf_op jit(solution)/shard_map/pallas_call | solution.py:549
  41.0 1.7 %shard_map.209 = (bf16[6,12,2,384]{3,2,1,0:T(2,128)(2,1)}, bf16[6,12,2,384]{3,2,1,0:T(2,128)(2,1)}, f32[384]{0:T(512)}, f32[24,72]{1,0:T(8,128)}, f32[24,24]{1,0:T(8,128)}, /*index=5*/f32[12,2,207]{2,1,0:T(2,128)}) custom-call(bf16[6,12,2,384]{3,2,1,0:T(2,128)(2,1)} %get-tuple-element.18.refs_0_, bf16[6,12,2,384]{3,2,1,0:T(2,128)(2,1)} %get-tuple-element.19.refs_1_, ...), custom_call_target="tpu_custom_call" | custom-call | tf_op jit(solution)/shard_map/pallas_call | solution.py:620

commit v4 on v3

--- a/solution.py
+++ b/solution.py
@@ -83,8 +83,8 @@
     gain_ref, wqkv, wproj, table, region_ref = rest[15:20]
     const = rest[20:29]
     (
-        win, win_cot, res, res_cot, out_own, gin_own, tok, keys, trow, amat, bias, probs, gsb, gqk, gv, att,
-        hs_own, hs_out, hs_in, as_own, as_out, as_in, gqk_in, gv_in, cw, cw_in,
+        win, win_cot, res, res_cot, out_own, gin_own, tok, keys, trow, amat, bias, probs, gsb, gqk, agv, hid,
+        gqk_in, agv_in, hid_in, cw, cw_in,
         ysend, yrecv, zsend, zrecv, xsend, xrecv, lsend, lrecv, bsend, brecv, asend, arecv,
         load_sem, own_sem, halo_s, halo_r, back_s, back_r, sib_s, sib_r, y_s, y_r, z_s, z_r, x_s, x_r,
         l_s, l_r, b_s, b_r, a_s, a_r,
@@ -107,13 +107,9 @@
     barrier = pltpu.get_barrier_semaphore()
     for dev in ((up, left), (down, right)):
         pl.semaphore_signal(barrier, inc=1, device_id=dev, device_id_type=MESH)
-
-    def greet(d, carry):
+    for d in (15, 1, *range(2, 15)):
         pl.semaphore_signal(barrier, inc=1, device_id=((i + d) % 16, j), device_id_type=MESH)
         pl.semaphore_signal(barrier, inc=1, device_id=(i, (j + d) % 16), device_id_type=MESH)
-        return carry
-
-    lax.fori_loop(1, 16, greet, 0)
 
     own = [
         pltpu.make_async_copy(s.at[3:6, 6:12], d.at[3:6, 6:12], own_sem.at[n])
@@ -207,22 +203,21 @@
     to_sib = [
         remote(src, dst, sib_s.at[n], sib_r.at[n], sibling)
         for n, (src, dst) in enumerate(
-            [(cw, cw_in), (hs_out, hs_in), (as_out, as_in), (gv, gv_in)]
+            [(cw, cw_in), (hid, hid_in)]
+            + [(agv.at[g], agv_in.at[g]) for g in range(3)]
             + [(gqk.at[g], gqk_in.at[g]) for g in range(3)]
         )
     ]
 
-    def split_halves(value, own_half, out_half):
-        spread = dot(halves[...], value, 1, 1).astype(BF16)
-        first, second = spread[0:192], spread[192:384]
-        own_half[...] = jnp.where(core == 0, first, second)
-        out_half[...] = jnp.where(core == 0, second, first)
+    def own_half(value):
+        picked = halves[pl.ds(pl.multiple_of(192 * core, 192), 192), :]
+        return dot(picked, value, 1, 1).astype(BF16)
 
     def whole(ref, ssem, rsem):
         return [pltpu.make_async_copy(ref, ref, sem) for sem in (ssem, rsem)]
 
     def weight_part(n, left_own, left_in, right_own, right_in):
-        part = dot(left_own[...], right_own) + dot(left_in[...], right_in)
+        part = dot(left_own, right_own) + dot(left_in, right_in)
         if n >= 2:
             q = n - 2
             for k in range(8):
@@ -294,9 +289,10 @@
     inv_std = lax.rsqrt(jnp.mean(jnp.square(shifted), 1, keepdims=True) + 1e-05)
     normed = shifted * inv_std
     hidden = (normed * gain).astype(BF16)
+    hid[...] = hidden
+    to_sib[1].start()
     joined = dot(hidden, wqkv[...]).astype(BF16)
-    split_halves(hidden, hs_own, hs_out)
-    to_sib[1].start()
+    hidden_own = own_half(hidden)
     own[1].wait()
     for c in halo[3:6]:
         c.wait_recv()
@@ -327,23 +323,26 @@
         weights = weights * (1.0 / jnp.sum(weights, 1, keepdims=True))
         probs[g] = weights
         probs_low = weights.astype(BF16)
-        att[:, lanes] = pick(dot(probs_low, value_part)).astype(BF16)
+        agv[g, :, 0:128] = pick(dot(probs_low, value_part)).astype(BF16)
         grad4 = jnp.concatenate([grad_att[:, lanes] * k for k in head_masks], 0)
-        gv[:, lanes] = dot(probs_low, grad4, 0, 0).astype(BF16)
-    to_sib[3].start()
-    attended = att[...]
-    split_halves(attended, as_own, as_out)
-    to_sib[2].start()
+        agv[g, :, 128:256] = dot(probs_low, grad4, 0, 0).astype(BF16)
+        to_sib[2 + g].start()
+    attended = jnp.concatenate([agv[g, :, 0:128] for g in range(3)], 1)
+    grad_values = jnp.concatenate([agv[g, :, 128:256] for g in range(3)], 1)
+    attended_own = own_half(attended)
+    to_sib[1].wait_recv()
+    hidden_in = own_half(hid_in[...])
 
     result = (wide + dot(attended, wproj[...])).astype(BF16)
     back_out = put_back(result, res, 0)
 
-    to_sib[1].wait_recv()
-    to_sib[3].wait_recv()
-    y_copies = [weight_part(0, hs_own, hs_in, gv[...], gv_in[...])]
+    for g in range(3):
+        to_sib[2 + g].wait_recv()
+    values_in = jnp.concatenate([agv_in[g, :, 128:256] for g in range(3)], 1)
+    y_copies = [weight_part(0, hidden_own, hidden_in, grad_values, values_in)]
     to_sib[0].wait_recv()
-    to_sib[2].wait_recv()
-    y_copies.append(weight_part(1, as_own, as_in, cw[...], cw_in[...]))
+    attended_in = own_half(jnp.concatenate([agv_in[g, :, 0:128] for g in range(3)], 1))
+    y_copies.append(weight_part(1, attended_own, attended_in, cw[...], cw_in[...]))
     for g in range(3):
         lanes = slice(128 * g, 128 * g + 128)
         queries4 = jnp.concatenate([joined[:, lanes] * k for k in head_masks], 0)
@@ -362,13 +361,13 @@
         grad_keys = dot(grad_scaled, queries4, 0, 0)
         gqk[g, :, 0:128] = grad_query.astype(BF16)
         gqk[g, :, 128:256] = grad_keys.astype(BF16)
-        to_sib[4 + g].start()
+        to_sib[5 + g].start()
         if g > 0:
-            to_sib[3 + g].wait_recv()
-            y_copies.append(weight_part(1 + g, hs_own, hs_in, gqk[g - 1], gqk_in[g - 1]))
+            to_sib[4 + g].wait_recv()
+            y_copies.append(weight_part(1 + g, hidden_own, hidden_in, gqk[g - 1], gqk_in[g - 1]))
 
     grad_joined = jnp.concatenate(
-        [gqk[g, :, 128 * n : 128 * n + 128] for n in range(2) for g in range(3)] + [gv[...]], 1
+        [gqk[g, :, 128 * n : 128 * n + 128] for n in range(2) for g in range(3)] + [grad_values], 1
     )
     grad_hidden = dot(grad_joined, wqkv[...], 1, 1)
     grad_gain = jnp.sum(grad_hidden * normed, 0, keepdims=True)
@@ -429,8 +428,8 @@
     all_lat = whole(arecv.at[pl.ds(1, 15)], a_s, a_r)
     start_all(bias_lon)
 
-    to_sib[6].wait_recv()
-    y_copies.append(weight_part(4, hs_own, hs_in, gqk[2], gqk_in[2]))
+    to_sib[7].wait_recv()
+    y_copies.append(weight_part(4, hidden_own, hidden_in, gqk[2], gqk_in[2]))
 
     mine, to_x = over_x()
     grad_normed = grad_hidden * gain
@@ -441,6 +440,19 @@
     )
     grad_in = (cot_rows.astype(F32) + grad_wide).astype(BF16)
     back_grad = put_back(grad_in, res_cot, 1)
+
+    all_bias[1].wait()
+    total = bsend[j].astype(F32)
+    for d in range(1, 16):
+        total = total + brecv[d].astype(F32)
+    kinds = total[15:16, 128:129] * (1.0 / 16.0)
+    block = jnp.where(share_row < 12, total, 0.0) + riders(gain_of(total), kinds)
+    asend[...] = block.astype(BF16)
+
+    def bias_lat(d):
+        return remote(asend, arecv.at[d], a_s, a_r, ((i + d) % 16, j))
+
+    start_all(bias_lat)
 
     own_qk = []
     for q in range(3):
@@ -475,24 +487,19 @@
 
     start_all(to_lon)
 
-    all_bias[1].wait()
-    total = bsend[j].astype(F32)
-    for d in range(1, 16):
-        total = total + brecv[d].astype(F32)
-    kinds = total[15:16, 128:129] * (1.0 / 16.0)
-    block = jnp.where(share_row < 12, total, 0.0) + riders(gain_of(total), kinds)
-    asend[...] = block.astype(BF16)
-
-    def bias_lat(d):
-        return remote(asend, arecv.at[d], a_s, a_r, ((i + d) % 16, j))
-
-    start_all(bias_lat)
 
     for c in (*halo, *to_sib, *back_out, *back_grad, to_x):
         c.wait_send()
     for sent, _ in y_copies:
         sent.wait()
     all_bias[0].wait()
+
+    writes = []
+    for n, (copies, target) in enumerate(((back_out, out_ref), (back_grad, gin_ref))):
+        for c in copies:
+            c.wait_recv()
+        writes.append(pltpu.make_async_copy(landed[n], target, own_sem.at[2 + n]))
+        writes[n].start()
 
     all_lat[1].wait()
     gain_total = jnp.zeros((1, 384), F32)
@@ -509,12 +516,6 @@
         row = jnp.concatenate([sums[0][h : h + 1, 0:207], sums[1][h : h + 1, 0:207]], 0)
         gbias_ref[h] = row
     all_lat[0].wait()
-    writes = []
-    for n, (copies, target) in enumerate(((back_out, out_ref), (back_grad, gin_ref))):
-        for c in copies:
-            c.wait_recv()
-        writes.append(pltpu.make_async_copy(landed[n], target, own_sem.at[2 + n]))
-        writes[n].start()
 
     all_lon[1].wait()
     total = lsend[j].astype(F32)
@@ -574,14 +575,9 @@
             pltpu.VMEM((3, 576, 144), F32),
             pltpu.VMEM((6, 288, 144), F32),
             pltpu.VMEM((3, 144, 256), BF16),
+            pltpu.VMEM((3, 144, 256), BF16),
             pltpu.VMEM((144, 384), BF16),
-            pltpu.VMEM((144, 384), BF16),
-            pltpu.VMEM((192, 144), BF16),
-            pltpu.VMEM((192, 144), BF16),
-            pltpu.VMEM((192, 144), BF16),
-            pltpu.VMEM((192, 144), BF16),
-            pltpu.VMEM((192, 144), BF16),
-            pltpu.VMEM((192, 144), BF16),
+            pltpu.VMEM((3, 144, 256), BF16),
             pltpu.VMEM((3, 144, 256), BF16),
             pltpu.VMEM((144, 384), BF16),
             pltpu.VMEM((144, 384), BF16),
@@ -599,7 +595,7 @@
             pltpu.VMEM((16, 256), BF16),
             pltpu.VMEM((16, 16, 256), BF16),
             dma((len(consts) + 5,)), dma((4,)),
-            dma((6,)), dma((6,)), dma((6,)), dma((6,)), dma((7,)), dma((7,)),
+            dma((6,)), dma((6,)), dma((6,)), dma((6,)), dma((8,)), dma((8,)),
             dma((2,)), dma((2,)), dma((3,)), dma((3,)), dma, dma,
             dma, dma, dma, dma, dma, dma,
         ],

time: 42.8 us -> 41.5 us (0.970)
  Pallas kernels: 41.4 us -> 40.1 us
    pallas_call x1, Pallas kernels: 39.7 us -> 38.4 us  [local(): pl.pallas_call(kernel, out_shape=shapes, in_specs=[hbm] * 7 + [pl.BlockSp...]
where the time goes in v4:
time: 41.5 us; the launch traced here: 41.4 us
  Pallas kernels  40.1 us (97%)
  between operations  1.29 us (3%)
    pallas_call x1, Pallas kernels, local(): pl.pallas_call(kernel, out_shape=shapes, in_specs=[hbm] * 7 + [pl.BlockSp...  38.4 us
    pallas_call x1, Pallas kernels, local(): pl.pallas_call(finish, out_shape=shapes, in_specs=[vmem] * 6, out_specs=[...  1.73 us

profile of v4, /device:TPU:1, one launch (start us, length us, event | category | flops | bytes accessed | tf_op | source)
XLA Modules:
  0.0 41.4 jit_solution(11761179786661991612)
XLA Ops:
  1.3 38.4 %shard_map.208 = (bf16[6,12,2,384]{3,2,1,0:T(2,128)(2,1)}, bf16[6,12,2,384]{3,2,1,0:T(2,128)(2,1)}, f32[384]{0:T(512)}, f32[24,72]{1,0:T(8,128)}, f32[24,24]{1,0:T(8,128)}, /*index=5*/f32[12,2,207]{2,1,0:T(2,128)}) custom-call(bf16[6,12,2,384]{3,2,1,0:T(2,128)(2,1)} %bitcast.8, bf16[6,12,2,384]{3,2,1,0:T(2,128)(2,1)} %bitcast.9, f32[384]{0:T(512)} %gain_hbm.1, ...), custom_call_target="tpu_custom_call" | custom-call | tf_op jit(solution)/shard_map/pallas_call | solution.py:550
  39.6 1.7 %shard_map.209 = (bf16[6,12,2,384]{3,2,1,0:T(2,128)(2,1)}, bf16[6,12,2,384]{3,2,1,0:T(2,128)(2,1)}, f32[384]{0:T(512)}, f32[24,72]{1,0:T(8,128)}, f32[24,24]{1,0:T(8,128)}, /*index=5*/f32[12,2,207]{2,1,0:T(2,128)}) custom-call(bf16[6,12,2,384]{3,2,1,0:T(2,128)(2,1)} %get-tuple-element.18.refs_0_, bf16[6,12,2,384]{3,2,1,0:T(2,128)(2,1)} %get-tuple-element.19.refs_1_, ...), custom_call_target="tpu_custom_call" | custom-call | tf_op jit(solution)/shard_map/pallas_call | solution.py:616

commit v5 on v4

--- a/solution.py
+++ b/solution.py
@@ -124,7 +124,7 @@
             )
         )
     ]
-    for c in (*own, *loads):
+    for c in (*own, *loads[:7]):
         c.start()
 
     corners = (
@@ -138,7 +138,11 @@
         for k, (spot, dev, _) in enumerate(corners)
     ]
     pl.semaphore_wait(barrier, 32)
-    for c in halo:
+    for c in halo[0:3]:
+        c.start()
+    for c in loads[7:]:
+        c.start()
+    for c in halo[3:6]:
         c.start()
 
     for c in loads[0:4]:
@@ -161,12 +165,11 @@
 
     kind = type_ref[0, 0]
     trow[...] = jnp.zeros((16, 3456), F32)
-    is_kind = lax.broadcasted_iota(jnp.int32, (32, 3312), 0) == kind
+    pick_col = lax.broadcasted_iota(jnp.int32, (16, 384), 1)
+    pick_row = lax.broadcasted_iota(jnp.int32, (16, 384), 0)
+    is_kind = ((pick_col == 32 * pick_row + kind) & (pick_row < 12)).astype(F32).astype(BF16)
     loads[4].wait()
-    for h in range(12):
-        trow[h : h + 1, 0:3312] = jnp.sum(
-            jnp.where(is_kind, table[h].astype(F32), 0.0), 0, keepdims=True
-        )
+    trow[:, 0:3312] = dot(is_kind, table[...].reshape(384, 3312))
     wide_lane = lax.broadcasted_iota(jnp.int32, (16, 384), 1)
     for zp in range(2):
         for ip in range(6):

time: 41.5 us -> 41.4 us (level)
  no operation moved by 1% of the time
where the time goes in v5:
time: 41.4 us; the launch traced here: 41.3 us
  Pallas kernels  40 us (97%)
  between operations  1.29 us (3%)
    pallas_call x1, Pallas kernels, local(): pl.pallas_call(kernel, out_shape=shapes, in_specs=[hbm] * 7 + [pl.BlockSp...  38.3 us
    pallas_call x1, Pallas kernels, local(): pl.pallas_call(finish, out_shape=shapes, in_specs=[vmem] * 6, out_specs=[...  1.73 us

profile of v5, /device:TPU:1, one launch (start us, length us, event | category | flops | bytes accessed | tf_op | source)
XLA Modules:
  0.0 41.3 jit_solution(18348176205950376851)
XLA Ops:
  1.3 38.3 %shard_map.208 = (bf16[6,12,2,384]{3,2,1,0:T(2,128)(2,1)}, bf16[6,12,2,384]{3,2,1,0:T(2,128)(2,1)}, f32[384]{0:T(512)}, f32[24,72]{1,0:T(8,128)}, f32[24,24]{1,0:T(8,128)}, /*index=5*/f32[12,2,207]{2,1,0:T(2,128)}) custom-call(bf16[6,12,2,384]{3,2,1,0:T(2,128)(2,1)} %bitcast.8, bf16[6,12,2,384]{3,2,1,0:T(2,128)(2,1)} %bitcast.9, f32[384]{0:T(512)} %gain_hbm.1, ...), custom_call_target="tpu_custom_call" | custom-call | tf_op jit(solution)/shard_map/pallas_call | solution.py:553
  39.6 1.7 %shard_map.209 = (bf16[6,12,2,384]{3,2,1,0:T(2,128)(2,1)}, bf16[6,12,2,384]{3,2,1,0:T(2,128)(2,1)}, f32[384]{0:T(512)}, f32[24,72]{1,0:T(8,128)}, f32[24,24]{1,0:T(8,128)}, /*index=5*/f32[12,2,207]{2,1,0:T(2,128)}) custom-call(bf16[6,12,2,384]{3,2,1,0:T(2,128)(2,1)} %get-tuple-element.18.refs_0_, bf16[6,12,2,384]{3,2,1,0:T(2,128)(2,1)} %get-tuple-element.19.refs_1_, ...), custom_call_target="tpu_custom_call" | custom-call | tf_op jit(solution)/shard_map/pallas_call | solution.py:619
